TPU v7x, 256 devices: a whole 4x4x8 slice. The times are simulated.
256 devices in a mesh: tm: 16 (over z, core), tile: 16 (over y, x).
Axes of the slice: x: 4, y: 4, z: 8, core: 2. Of those that a mesh axis runs over, the one named last changes fastest.
Arguments:
- boundary_inv: float32 [16, 1024, 1024], P('tm', 'tile'), may hold values from -1 to 1, as said below
- coupling: bfloat16 [16, 1024, 1024], P('tm', 'tile'), may hold values from -2 to 2
- interior_map: bfloat16 [16, 4, 1024, 1024], P('tm'), may hold values from -0.1875 to 0.1875
- interior_inv: float32 [16, 4, 1024, 1024], P('tm', None, 'tile'), may hold values from -1 to 2, as said below
Outputs:
- boundary_cov: float32 [16, 1024, 1024], P('tm', 'tile')
- interior_cov: float32 [16, 4, 1024, 1024], P('tm', None, 'tile')
Inputs may be any that keep to these rules, and one draw needn't show every extreme that they name: `boundary_inv`: each block is symmetric. `interior_inv`: each block is symmetric.
All inputs are finite; a program needn't handle non-finite values.
Results may differ from a plain program's by a relative error of at most 0.0041.
Values may be sent and summed in bfloat16 or wider, within the bound.
No kernel may reach another device: no remote copies, remote signals or barrier semaphores. Data moves between devices by JAX's collectives and lax.ppermute only.
A program may use at most 64 MiB of HBM per device.

v0:
```python
import jax
import jax.numpy as jnp
from jax import lax
from jax.sharding import PartitionSpec as P


def shifted(value, axis, by):
    peers = lax.axis_size(axis)
    pairs = [(i, i + by) for i in range(peers) if 0 <= i + by < peers]
    return lax.ppermute(value, axis, pairs)


def gather_factor(factor):
    return lax.all_gather(factor, "tile", axis=0, tiled=True)


def fold_level(sigma_rows, whole_factor, partner_rows, row_start, row_count):
    product = jnp.dot(partner_rows, whole_factor, preferred_element_type=jnp.float32).astype(
        jnp.bfloat16
    )
    own_cols = lax.dynamic_slice_in_dim(whole_factor, row_start, row_count, 1)
    return sigma_rows + lax.dot_general(
        own_cols,
        lax.all_gather(product, "tile", axis=0, tiled=True),
        (((0,), (0,)), ((), ())),
        preferred_element_type=jnp.float32,
    )


def shards(boundary_inv, coupling, interior_map, interior_inv):
    levels = lax.axis_size("tm").bit_length() - 1
    row_count = boundary_inv.shape[1]
    row_start = lax.axis_index("tile") * row_count
    sigma_rows = boundary_inv[0]
    factor = coupling[0]
    whole_factor = gather_factor(factor)
    for height in range(levels):
        stride = 2**height
        if height + 1 < levels:
            stacked = jnp.stack([sigma_rows.astype(jnp.bfloat16), factor])
            moved = shifted(stacked, "tm", -stride)
            sigma_rows = fold_level(sigma_rows, whole_factor, moved[0], row_start, row_count)
            factor = jnp.dot(moved[1], whole_factor, preferred_element_type=jnp.float32).astype(
                jnp.bfloat16
            )
            whole_factor = gather_factor(factor)
        else:
            moved_rows = shifted(sigma_rows.astype(jnp.bfloat16), "tm", -stride)
            sigma_rows = fold_level(sigma_rows, whole_factor, moved_rows, row_start, row_count)
    sigma_low = sigma_rows.astype(jnp.bfloat16)
    maps = interior_map[0]
    own_maps = lax.dynamic_slice_in_dim(maps, row_start, row_count, 2)
    whole_sigma = lax.all_gather(sigma_low, "tile", axis=0, tiled=True)
    full_rows = jnp.einsum(
        "ab,jbc->jac", whole_sigma, maps, preferred_element_type=jnp.float32
    ).astype(jnp.bfloat16)
    interior_cov = interior_inv[0] + jnp.einsum(
        "jbr,jbc->jrc", own_maps, full_rows, preferred_element_type=jnp.float32
    )
    return (sigma_rows[None], interior_cov[None])


def solution(mesh):
    in_specs = (
        P("tm", "tile", None),
        P("tm", "tile", None),
        P("tm", None, None, None),
        P("tm", None, "tile", None),
    )
    out_specs = (P("tm", "tile", None), P("tm", None, "tile", None))
    return jax.shard_map(shards, mesh=mesh, in_specs=in_specs, out_specs=out_specs, check_vma=False)
```

profile of v0, /device:TPU:1, one launch (start us, length us, event | category | flops | bytes accessed | tf_op | source)
XLA Modules:
  0.0 503.5 jit_solution(3238245929460345960)
XLA Ops:
  9.9 5.3 %collective-permute-start = (bf16[2,64,1024]{2,1,0:T(8,128)(2,1)S(1)}, bf16[2,64,1024]{2,1,0:T(8,128)(2,1)S(1)}, u32[]{:S(2)}, u32[]{:S(2)}) collective-permute-start(bf16[2,64,1024]{2,1,0:T(8,128)(2,1)S(1)} %pad_maximum_fusion), channel_id=1, source_target_pairs={{16,0},{32,16},{48,32},{64,48},{80,64},{96,80},{112,96},{128,112},... | collective-permute-start | bytes 786440 | tf_op jit(solution)/shard_map/ppermute | solution.py:10
  15.2 3.8 collective-permute-done
  19.0 44.4 %all-gather.27.cloned.1.call-done = bf16[1,1024,1024]{2,1,0:T(8,128)(2,1)} async-done(((bf16[1,64,1024]{2,1,0:T(8,128)(2,1)}), bf16[1,1024,1024]{2,1,0:T(8,128)(2,1)}) %all-gather.27.cloned.1.call-update) | async-done | bytes 2097168 | tf_op jit(solution)/shard_map/all_gather | solution.py:14
  63.4 2.9 fusion.32
  67.6 48.2 %all-gather.11.cloned.1.call-done = bf16[1024,1024]{1,0:T(8,128)(2,1)} async-done(((bf16[64,1024]{1,0:T(8,128)(2,1)}), bf16[1024,1024]{1,0:T(8,128)(2,1)}) %all-gather.11.cloned.1.call-update) | async-done | bytes 2097168 | tf_op jit(solution)/shard_map/all_gather | solution.py:24
  115.8 2.2 convolution_add_fusion.3
  118.1 1.3 collective-permute-start.1
  119.4 48.8 %all-gather.13.cloned.1.call-done = bf16[1024,1024]{1,0:T(8,128)(2,1)} async-done(((bf16[64,1024]{1,0:T(8,128)(2,1)}), bf16[1024,1024]{1,0:T(8,128)(2,1)}) %all-gather.13.cloned.1.call-update) | async-done | bytes 2097168 | tf_op jit(solution)/shard_map/all_gather | solution.py:14
  168.2 2.9 convolution_convert_fusion.4
  172.4 48.2 %all-gather.15.cloned.1.call-done = bf16[1024,1024]{1,0:T(8,128)(2,1)} async-done(((bf16[64,1024]{1,0:T(8,128)(2,1)}), bf16[1024,1024]{1,0:T(8,128)(2,1)}) %all-gather.15.cloned.1.call-update) | async-done | bytes 2097168 | tf_op jit(solution)/shard_map/all_gather | solution.py:24
  220.6 2.2 convolution_add_fusion.2
  222.9 1.3 collective-permute-start.2
  224.2 48.7 %all-gather.17.cloned.1.call-done = bf16[1024,1024]{1,0:T(8,128)(2,1)} async-done(((bf16[64,1024]{1,0:T(8,128)(2,1)}), bf16[1024,1024]{1,0:T(8,128)(2,1)}) %all-gather.17.cloned.1.call-update) | async-done | bytes 2097168 | tf_op jit(solution)/shard_map/all_gather | solution.py:14
  272.9 2.9 convolution_convert_fusion.2
  275.8 1.1 convolution_convert_fusion.1
  277.1 48.2 %all-gather.19.cloned.1.call-done = bf16[1024,1024]{1,0:T(8,128)(2,1)} async-done(((bf16[64,1024]{1,0:T(8,128)(2,1)}), bf16[1024,1024]{1,0:T(8,128)(2,1)}) %all-gather.19.cloned.1.call-update) | async-done | bytes 2097168 | tf_op jit(solution)/shard_map/all_gather | solution.py:24
  325.3 2.2 fusion.47
  327.5 1.3 collective-permute-start.3
  328.8 48.9 %all-gather.21.cloned.1.call-done = bf16[1024,1024]{1,0:T(8,128)(2,1)} async-done(((bf16[64,1024]{1,0:T(8,128)(2,1)}), bf16[1024,1024]{1,0:T(8,128)(2,1)}) %all-gather.21.cloned.1.call-update) | async-done | bytes 2097168 | tf_op jit(solution)/shard_map/all_gather | solution.py:14
  377.7 2.7 convolution_convert_fusion
  380.5 49.6 %all-gather.23.cloned.1.call-done = bf16[1024,1024]{1,0:T(8,128)(2,1)} async-done(((bf16[64,1024]{1,0:T(8,128)(2,1)}), bf16[1024,1024]{1,0:T(8,128)(2,1)}) %all-gather.23.cloned.1.call-update) | async-done | bytes 2097168 | tf_op jit(solution)/shard_map/all_gather | solution.py:24
  430.1 3.1 fusion.48
  433.2 49.5 %all-gather.25.cloned.1.call-done = bf16[1024,1024]{1,0:T(8,128)(2,1)} async-done(((bf16[64,1024]{1,0:T(8,128)(2,1)}), bf16[1024,1024]{1,0:T(8,128)(2,1)}) %all-gather.25.cloned.1.call-update) | async-done | bytes 2097168 | tf_op jit(solution)/shard_map/all_gather | solution.py:53
  482.7 14.3 %fusion.22 = f32[1,4,64,1024]{3,2,1,0:T(8,128)} fusion(bf16[1,4,1024,1024]{3,2,1,0:T(8,128)(2,1)} %param.6, bf16[1024,1024]{1,0:T(8,128)(2,1)} %all-gather.25.cloned.1.call-done, f32[1,4,64,1024]{3,2,1,0:T(8,128)S(1)} %copy-done.6, s32[]{:T(128)S(6)} %select_n.2), kind=kOutput, calls=%fused_computation.11 | convolution fusion | flops 9131261952 | bytes 13631492 | tf_op jit(solution)/shard_map/jbr,jbc->jrc/dot_general | solution.py:57
  (43 shorter events, 5.5 us)
Async XLA Ops:
  7.2 56.2 %all-gather.27.cloned.1.call-start = ((), (), s32[]{:S(2)}) async-start(), calls=%async_computation.8 | async-start | bytes 2228224 | tf_op jit(solution)/shard_map/all_gather | solution.py:14
  7.9 107.9 %all-gather.11.cloned.1.call-start = ((), (), s32[]{:S(2)}) async-start(), calls=%async_computation | async-start | bytes 2228224 | tf_op jit(solution)/shard_map/all_gather | solution.py:24
  9.8 105.9 %copy-start.5 = (f32[1,64,1024]{2,1,0:T(8,128)S(1)}, f32[1,64,1024]{2,1,0:T(8,128)}, u32[]{:S(2)}) copy-start(f32[1,64,1024]{2,1,0:T(8,128)} %param.4) | copy-start | bytes 786436
  9.9 9.1 %collective-permute-start = (bf16[2,64,1024]{2,1,0:T(8,128)(2,1)S(1)}, bf16[2,64,1024]{2,1,0:T(8,128)(2,1)S(1)}, u32[]{:S(2)}, u32[]{:S(2)}) collective-permute-start(bf16[2,64,1024]{2,1,0:T(8,128)(2,1)S(1)} %pad_maximum_fusion), channel_id=1, source_target_pairs={{16,0},{32,16},{48,32},{64,48},{80,64},{96,80},{112,96},{128,112},... | collective-permute-start | bytes 786440 | tf_op jit(solution)/shard_map/ppermute | solution.py:10
  63.4 3.0 copy-start.1
  66.3 101.9 %all-gather.13.cloned.1.call-start = ((), (), s32[]{:S(2)}) async-start(), calls=%async_computation.1 | async-start | bytes 2228224 | tf_op jit(solution)/shard_map/all_gather | solution.py:14
  67.5 50.6 %copy-start.3 = (bf16[64,1024]{1,0:T(8,128)(2,1)S(1)}, bf16[64,1024]{1,0:T(8,128)(2,1)}, u32[]{:S(2)}) copy-start(bf16[64,1024]{1,0:T(8,128)(2,1)} %fusion.29) | copy-start | bytes 393220
  67.5 153.1 %all-gather.15.cloned.1.call-start = ((), (), s32[]{:S(2)}) async-start(), calls=%async_computation.2 | async-start | bytes 2228224 | tf_op jit(solution)/shard_map/all_gather | solution.py:24
  118.1 50.1 %collective-permute-start.1 = (bf16[2,64,1024]{2,1,0:T(8,128)(2,1)S(1)}, bf16[2,64,1024]{2,1,0:T(8,128)(2,1)S(1)}, u32[]{:S(2)}, u32[]{:S(2)}) collective-permute-start(bf16[2,64,1024]{2,1,0:T(8,128)(2,1)S(1)} %pad_maximum_fusion.1), channel_id=1, source_target_pairs={{32,0},{48,16},{64,32},{80,48},{96,64},{112,80},{128,96},{144,112}... | collective-permute-start | bytes 786440 | tf_op jit(solution)/shard_map/ppermute | solution.py:10
  168.2 3.0 copy-start
  171.1 101.8 %all-gather.17.cloned.1.call-start = ((), (), s32[]{:S(2)}) async-start(), calls=%async_computation.3 | async-start | bytes 2228224 | tf_op jit(solution)/shard_map/all_gather | solution.py:14
  172.3 50.6 %copy-start.4 = (bf16[64,1024]{1,0:T(8,128)(2,1)S(1)}, bf16[64,1024]{1,0:T(8,128)(2,1)}, u32[]{:S(2)}) copy-start(bf16[64,1024]{1,0:T(8,128)(2,1)} %convolution_convert_fusion.3) | copy-start | bytes 393220
  172.3 153.0 %all-gather.19.cloned.1.call-start = ((), (), s32[]{:S(2)}) async-start(), calls=%async_computation.4 | async-start | bytes 2228224 | tf_op jit(solution)/shard_map/all_gather | solution.py:24
  222.9 50.0 %collective-permute-start.2 = (bf16[2,64,1024]{2,1,0:T(8,128)(2,1)S(1)}, bf16[2,64,1024]{2,1,0:T(8,128)(2,1)S(1)}, u32[]{:S(2)}, u32[]{:S(2)}) collective-permute-start(bf16[2,64,1024]{2,1,0:T(8,128)(2,1)S(1)} %pad_maximum_fusion.2), channel_id=1, source_target_pairs={{64,0},{80,16},{96,32},{112,48},{128,64},{144,80},{160,96},{176,11... | collective-permute-start | bytes 786440 | tf_op jit(solution)/shard_map/ppermute | solution.py:10
  272.9 3.0 copy-start.2
  275.8 101.9 %all-gather.21.cloned.1.call-start = ((), (), s32[]{:S(2)}) async-start(), calls=%async_computation.5 | async-start | bytes 2228224 | tf_op jit(solution)/shard_map/all_gather | solution.py:14
  277.0 153.1 %all-gather.23.cloned.1.call-start = ((), (), s32[]{:S(2)}) async-start(), calls=%async_computation.6 | async-start | bytes 2228224 | tf_op jit(solution)/shard_map/all_gather | solution.py:24
  327.5 50.2 %collective-permute-start.3 = (bf16[64,1024]{1,0:T(8,128)(2,1)S(1)}, bf16[64,1024]{1,0:T(8,128)(2,1)S(1)}, u32[]{:S(2)}, u32[]{:S(2)}) collective-permute-start(bf16[64,1024]{1,0:T(8,128)(2,1)S(1)} %get-tuple-element.2), channel_id=1, source_target_pairs={{128,0},{144,16},{160,32},{176,48},{192,64},{208,80},{224,96},{240... | collective-permute-start | bytes 393224 | tf_op jit(solution)/shard_map/ppermute | solution.py:10
  380.4 102.3 %copy-start.6 = (f32[1,4,64,1024]{3,2,1,0:T(8,128)S(1)}, f32[1,4,64,1024]{3,2,1,0:T(8,128)}, u32[]{:S(2)}) copy-start(f32[1,4,64,1024]{3,2,1,0:T(8,128)} %param.7) | copy-start | bytes 3145732
  380.4 102.2 %all-gather.25.cloned.1.call-start = ((), (), s32[]{:S(2)}) async-start(), calls=%async_computation.7 | async-start | bytes 2228224 | tf_op jit(solution)/shard_map/all_gather | solution.py:53
Sparse Core Ops, SparseCore 0:
  10.4 52.8 all-gather.26
  66.4 49.3 all-gather.10
  118.8 49.3 all-gather.12
  171.2 49.3 all-gather.14
  223.5 49.3 all-gather.16
  275.9 49.3 all-gather.18
  328.3 49.3 all-gather.20
  380.7 49.3 all-gather.22
  433.3 49.3 all-gather.24
where the time goes:
time: 504 us; the launch traced here: 503 us
  waiting for transfers between devices  439 us (87%)
  matrix products  38.8 us (8%)
  between operations  14 us (3%)
  starting transfers between devices  9.52 us (2%)
    all_gather x4, waiting for transfers between devices, fold_level(): lax.all_gather(product, 'tile', axis=0, tiled=True)  194 us
    all_gather x4, waiting for transfers between devices, gather_factor(): return lax.all_gather(factor, 'tile', axis=0, tiled=True)  191 us
    all_gather x1, waiting for transfers between devices, shards(): whole_sigma = lax.all_gather(sigma_low, 'tile', axis=0, tiled=True)  49.5 us
    dot_general x1, matrix products, shards(): jnp.einsum('jbr,jbc->jrc', own_maps, full_rows, preferred_element_type=jn...  14.3 us
    dot_general x4, matrix products, fold_level(): jnp.dot(partner_rows, whole_factor, preferred_element_type=jnp.float32)  11.4 us
  transfers between devices with their start and end apart: 13, of which 10 were waited for; matrix products, arithmetic and copies ran while one was open for 2% of the time, Pallas kernels for 0%

commit v1 on v0

v1 whole, which is shorter than its diff:
```python
import jax
import jax.numpy as jnp
from jax import lax
from jax.experimental import pallas as pl
from jax.experimental.pallas import tpu as pltpu
from jax.sharding import PartitionSpec as P

AXES = ("tm", "tile")
BF16 = jnp.bfloat16
F32 = jnp.float32


def dot(left, right, left_dim, right_dim):
    return lax.dot_general(
        left, right, (((left_dim,), (right_dim,)), ((), ())), preferred_element_type=F32
    )


def interior_rows(sigma_ref, maps_ref, out_ref):
    sigma = sigma_ref[...]
    one, two = [
        jnp.dot(sigma, maps_ref[j], preferred_element_type=F32) for j in range(2)
    ]
    rows, width = out_ref.shape[1:]
    low = lax.broadcasted_iota(jnp.int32, (rows, width), 1) < width // 2
    for pair in range(out_ref.shape[0] // 2):
        a = one[:, pair * width : (pair + 1) * width]
        b = two[:, pair * width : (pair + 1) * width]
        even = jnp.where(low, a, pltpu.roll(b, width // 2, 1))
        odd = jnp.where(low, pltpu.roll(a, width // 2, 1), b)
        out_ref[2 * pair] = even.astype(BF16)
        out_ref[2 * pair + 1] = odd.astype(BF16)


def interior_sums(cols_ref, maps_ref, inv_ref, out_ref):
    rows = inv_ref.shape[1]
    turned = cols_ref[...].T
    for j in range(2):
        out_ref[j] = inv_ref[j] + jnp.dot(
            turned[j * rows : (j + 1) * rows], maps_ref[j], preferred_element_type=F32
        )


def shards(boundary_inv, coupling, interior_map, interior_inv):
    planes = lax.axis_size("tm") // 2
    tiles = lax.axis_size("tile")
    first = lax.axis_index("tm") % 2 == 0
    chunk, order = boundary_inv.shape[1:]
    half = order // 2

    def move(value, route):
        pairs = []
        for z in range(planes):
            for c in range(2):
                to = route(z, c)
                if to is not None and 0 <= to[0] < planes:
                    for t in range(tiles):
                        source, target = 2 * z + c, 2 * to[0] + to[1]
                        pairs.append((source * tiles + t, target * tiles + t))
        return lax.ppermute(value, AXES, pairs)

    def swap_cores(value):
        return move(value, lambda z, c: (z, 1 - c))

    def exchange(pieces):
        return lax.all_to_all(pieces, "tile", 0, 0)

    def gather(value):
        return exchange(jnp.broadcast_to(value, (tiles, *value.shape)))

    def times(left, left_dim, halves):
        mine, other = [dot(left, h, left_dim, 0) for h in halves]
        return jnp.concatenate(
            [jnp.where(first, mine, other), jnp.where(first, other, mine)], 1
        )

    def cut(value):
        pieces = value.reshape(chunk, tiles, chunk).swapaxes(0, 1)
        return jnp.concatenate([pieces, jnp.zeros_like(pieces)], 2)

    def turn(value):
        return exchange(cut(value)).reshape(order, 2 * chunk)[:, :chunk]

    b_rows = boundary_inv[0]
    f_rows = coupling[0]
    maps = interior_map[0]
    count = maps.shape[0]

    give = jnp.where(first, f_rows[:, half:], f_rows[:, :half])
    given = swap_cores(jnp.concatenate([b_rows.astype(BF16), give], 1))
    x_rows = jnp.where(first, given[:, :order], f_rows)
    even_half = jnp.where(first, f_rows[:, :half], given[:, order:])
    odd_half = jnp.where(first, given[:, order:], f_rows[:, half:])

    odd_mine = lax.all_gather(odd_half, "tile", axis=0, tiled=True)

    f_mine = gather(even_half).reshape(order, half)
    sigma = b_rows
    levels = planes.bit_length() - 1
    for level in range(levels + 1):
        last = level == levels
        if level:
            hop = 2 ** (level - 1)
            block = jnp.where(first, sigma.astype(BF16), product)
            x_rows = move(block, lambda z, c: None if last and c else (z - hop, c))
        halves = (f_mine, swap_cores(f_mine))
        product = times(x_rows, 1, halves).astype(BF16)
        if last:
            w_cols = turn(product)
        else:
            new_half = move(
                product[:, :half], lambda z, c: (z, 0) if c else None
            )
            new_half = jnp.where(first, new_half, product[:, half:])
            pieces = jnp.concatenate(
                [
                    jnp.broadcast_to(new_half, (tiles, chunk, half)),
                    cut(product),
                ],
                2,
            )
            pieces = exchange(pieces).reshape(order, half + 2 * chunk)
            w_cols = pieces[:, half : half + chunk]
            f_mine = pieces[:, :half]
        sigma = sigma + times(w_cols, 0, halves)

    low = sigma.astype(BF16)
    x_rows = move(low, lambda z, c: (z - 1, 1) if c == 0 else None)
    odd_other = move(odd_mine, lambda z, c: (z, 1) if c == 0 else None)
    halves = (odd_mine, odd_other)
    w_cols = turn(times(x_rows, 1, halves).astype(BF16))
    sigma = jnp.where(first, sigma, b_rows + times(w_cols, 0, halves))

    low = sigma.astype(BF16)
    params = pltpu.CompilerParams(vmem_limit_bytes=40 * 2**20)
    cost = pl.CostEstimate(
        flops=2 * count * chunk * order * order,
        bytes_accessed=2 * count * order * order,
        transcendentals=0,
    )
    v_rows = pl.pallas_call(
        interior_rows,
        grid=(count // 2,),
        in_specs=[
            pl.BlockSpec((chunk, order), lambda j: (0, 0)),
            pl.BlockSpec((2, order, order), lambda j: (j, 0, 0)),
        ],
        out_specs=pl.BlockSpec((tiles, chunk, 2 * chunk), lambda j: (0, 0, j)),
        out_shape=jax.ShapeDtypeStruct((tiles, chunk, count * chunk), BF16),
        compiler_params=params,
        cost_estimate=cost,
    )(low, maps)
    v_cols = exchange(v_rows).reshape(order, count * chunk)
    interior_cov = pl.pallas_call(
        interior_sums,
        grid=(count // 2,),
        in_specs=[
            pl.BlockSpec((order, 2 * chunk), lambda j: (0, j)),
            pl.BlockSpec((2, order, order), lambda j: (j, 0, 0)),
            pl.BlockSpec((2, chunk, order), lambda j: (j, 0, 0)),
        ],
        out_specs=pl.BlockSpec((2, chunk, order), lambda j: (j, 0, 0)),
        out_shape=jax.ShapeDtypeStruct((count, chunk, order), F32),
        compiler_params=params,
        cost_estimate=cost,
    )(v_cols, maps, interior_inv[0])
    return sigma[None], interior_cov[None]


def solution(mesh):
    in_specs = (
        P("tm", "tile", None),
        P("tm", "tile", None),
        P("tm", None, None, None),
        P("tm", None, "tile", None),
    )
    out_specs = (P("tm", "tile", None), P("tm", None, "tile", None))
    return jax.shard_map(shards, mesh=mesh, in_specs=in_specs, out_specs=out_specs, check_vma=False)
```

time: 504 us -> 243 us (0.48)
  waiting for transfers between devices: 439 us -> 77.5 us
  blocking collectives: 0 us -> 78.4 us
  matrix products: 38.8 us -> 8.55 us
  starting transfers between devices: 9.52 us -> 36.4 us
  local copies, waits for them, and re-layouts: 0.03 us -> 11.8 us
  Pallas kernels: 0 us -> 5.22 us
    all_gather x9 -> x1, waiting for transfers between devices: 435 us -> 23.6 us  [shards(): odd_mine = lax.all_gather(odd_half, 'tile', axis=0, tiled=True)]
    all_to_all x0 -> x4, blocking collectives: none -> 78.4 us  [exchange(): return lax.all_to_all(pieces, 'tile', 0, 0)]
    dot_general x12 -> x20, matrix products: 38.8 us -> 8.55 us  [dot(): lax.dot_general(left, right, (((left_dim,), (right_dim,)), ((), ())), pre...]
    all_to_all x0 -> x3, waiting for transfers between devices: none -> 28.8 us  [exchange(): return lax.all_to_all(pieces, 'tile', 0, 0)]
    ppermute x4 -> x13, waiting for transfers between devices: 3.84 us -> 24.4 us  [move(): return lax.ppermute(value, AXES, pairs)]
    ppermute x4 -> x13, starting transfers between devices: 9.16 us -> 25.4 us  [move(): return lax.ppermute(value, AXES, pairs)]
    all_to_all x0 -> x3, starting transfers between devices: none -> 10.9 us  [exchange(): return lax.all_to_all(pieces, 'tile', 0, 0)]
    unnamed x14 -> x50, local copies, waits for them, and re-layouts: 0.03 us -> 8.74 us
  transfers between devices with their start and end apart: 13 -> 17, of which waited for: 10 -> 13; matrix products, arithmetic and copies ran while one was open for 2% -> 2% of each run, Pallas kernels for 0% -> 0%
where the time goes in v1:
time: 243 us; the launch traced here: 239 us
  blocking collectives  78.4 us (32%)
  waiting for transfers between devices  77.5 us (32%)
  starting transfers between devices  36.4 us (15%)
  between operations  14.8 us (6%)
  local copies, waits for them, and re-layouts  11.8 us (5%)
  matrix products  8.55 us (4%)
  other arithmetic  6.84 us (3%)
  Pallas kernels  5.22 us (2%)
    all_to_all x4, blocking collectives, exchange(): return lax.all_to_all(pieces, 'tile', 0, 0)  78.4 us
    all_to_all x3, waiting for transfers between devices, exchange(): return lax.all_to_all(pieces, 'tile', 0, 0)  28.8 us
    ppermute x13, starting transfers between devices, move(): return lax.ppermute(value, AXES, pairs)  25.4 us
    ppermute x13, waiting for transfers between devices, move(): return lax.ppermute(value, AXES, pairs)  24.4 us
    all_gather x1, waiting for transfers between devices, shards(): odd_mine = lax.all_gather(odd_half, 'tile', axis=0, tiled=True)  23.6 us
    all_to_all x3, starting transfers between devices, exchange(): return lax.all_to_all(pieces, 'tile', 0, 0)  10.9 us
    unnamed x50, local copies, waits for them, and re-layouts  8.74 us
    dot_general x20, matrix products, dot(): lax.dot_general(left, right, (((left_dim,), (right_dim,)), ((), ())), pre...  8.55 us
  transfers between devices with their start and end apart: 17, of which 13 were waited for; matrix products, arithmetic and copies ran while one was open for 2% of the time, Pallas kernels for 0%

profile of v1, /device:TPU:1, one launch (start us, length us, event | category | flops | bytes accessed | tf_op | source)
XLA Modules:
  0.0 239.5 jit_solution(10289459606660296005)
XLA Ops:
  9.1 3.3 %collective-permute-start = (bf16[64,1536]{1,0:T(8,128)(2,1)S(1)}, bf16[64,1536]{1,0:T(8,128)(2,1)S(1)}, u32[]{:S(2)}, u32[]{:S(2)}) collective-permute-start(bf16[64,1536]{1,0:T(8,128)(2,1)S(1)} %pad_maximum_fusion), channel_id=1, source_target_pairs={{0,16},{1,17},{2,18},{3,19},{4,20},{5,21},{6,22},{7,23},{8,24},{9,... | collective-permute-start | bytes 589832 | tf_op jit(solution)/shard_map/ppermute | solution.py:60
  15.1 21.3 %all_to_all.35 = bf16[16,64,512]{2,1,0:T(8,128)(2,1)S(1)} all-to-all(bf16[16,64,512]{2,1,0:T(8,128)(2,1)S(1)} %broadcast_in_dim.16), channel_id=1, replica_groups=mesh['tm'=16,'tile'=16] {'tile'}, dimensions={0} | all-to-all | bytes 2097152 | tf_op jit(solution)/shard_map/all_to_all | solution.py:66
  36.4 1.8 collective-permute-start.1
  38.1 2.3 collective-permute-done.1
  41.4 2.3 collective-permute-start.2
  45.3 22.1 %all_to_all.36 = bf16[16,64,640]{2,1,0:T(8,128)(2,1)S(1)} all-to-all(bf16[16,64,640]{2,1,0:T(8,128)(2,1)S(1)} %maximum_maximum_fusion), channel_id=1, replica_groups=mesh['tm'=16,'tile'=16] {'tile'}, dimensions={0} | all-to-all | bytes 2621440 | tf_op jit(solution)/shard_map/all_to_all | solution.py:66
  67.5 1.5 collective-permute-start.4
  71.1 5.3 %collective-permute-done.3 = bf16[64,1024]{1,0:T(8,128)(2,1)S(1)} collective-permute-done((bf16[64,1024]{1,0:T(8,128)(2,1)S(1)}, bf16[64,1024]{1,0:T(8,128)(2,1)S(1)}, u32[]{:S(2)}, u32[]{:S(2)}) %collective-permute-start.3) | collective-permute-done | bytes 131104 | tf_op jit(solution)/shard_map/ppermute | solution.py:60
  77.3 3.3 %collective-permute-start.5 = (bf16[64,512]{1,0:T(8,128)(2,1)S(1)}, bf16[64,512]{1,0:T(8,128)(2,1)S(1)}, u32[]{:S(2)}, u32[]{:S(2)}) collective-permute-start(bf16[64,512]{1,0:T(8,128)(2,1)S(1)} %get-tuple-element.28), channel_id=1, source_target_pairs={{16,0},{17,1},{18,2},{19,3},{20,4},{21,5},{22,6},{23,7},{24,8},{25... | collective-permute-start | bytes 196616 | tf_op jit(solution)/shard_map/ppermute | solution.py:60
  82.2 22.1 %all_to_all.37 = bf16[16,64,640]{2,1,0:T(8,128)(2,1)S(1)} all-to-all(bf16[16,64,640]{2,1,0:T(8,128)(2,1)S(1)} %maximum_maximum_fusion.1), channel_id=1, replica_groups=mesh['tm'=16,'tile'=16] {'tile'}, dimensions={0} | all-to-all | bytes 2621440 | tf_op jit(solution)/shard_map/all_to_all | solution.py:66
  108.0 6.8 %collective-permute-done.6 = bf16[64,1024]{1,0:T(8,128)(2,1)S(1)} collective-permute-done((bf16[64,1024]{1,0:T(8,128)(2,1)S(1)}, bf16[64,1024]{1,0:T(8,128)(2,1)S(1)}, u32[]{:S(2)}, u32[]{:S(2)}) %collective-permute-start.6) | collective-permute-done | bytes 131104 | tf_op jit(solution)/shard_map/ppermute | solution.py:60
  115.7 4.4 %collective-permute-start.8 = (bf16[64,512]{1,0:T(8,128)(2,1)S(1)}, bf16[64,512]{1,0:T(8,128)(2,1)S(1)}, u32[]{:S(2)}, u32[]{:S(2)}) collective-permute-start(bf16[64,512]{1,0:T(8,128)(2,1)S(1)} %get-tuple-element.30), channel_id=1, source_target_pairs={{16,0},{17,1},{18,2},{19,3},{20,4},{21,5},{22,6},{23,7},{24,8},{25... | collective-permute-start | bytes 196616 | tf_op jit(solution)/shard_map/ppermute | solution.py:60
  123.3 3.7 %all-to-all-start.3 = ((bf16[16,64,640]{2,1,0:T(8,128)(2,1)}), bf16[16,64,640]{2,1,0:T(8,128)(2,1)S(1)}, u32[]{:S(2)}, u32[]{:S(2)}) async-start(bf16[16,64,640]{2,1,0:T(8,128)(2,1)} %maximum_maximum_fusion.2), calls=%async_computation.3 | async-start | bytes 2621440 | tf_op jit(solution)/shard_map/all_to_all | solution.py:66
  127.7 20.7 %all-to-all-done.3 = bf16[16,64,640]{2,1,0:T(8,128)(2,1)S(1)} async-done(((bf16[16,64,640]{2,1,0:T(8,128)(2,1)}), bf16[16,64,640]{2,1,0:T(8,128)(2,1)S(1)}, u32[]{:S(2)}, u32[]{:S(2)}) %all-to-all-start.3) | async-done | bytes 1310752 | tf_op jit(solution)/shard_map/all_to_all | solution.py:66
  154.2 3.5 %all-to-all-start.4 = ((bf16[16,64,128]{2,1,0:T(8,128)(2,1)}), bf16[16,64,128]{2,1,0:T(8,128)(2,1)S(1)}, u32[]{:S(2)}, u32[]{:S(2)}) async-start(bf16[16,64,128]{2,1,0:T(8,128)(2,1)} %concatenate.153), calls=%async_computation.4 | async-start | bytes 524288 | tf_op jit(solution)/shard_map/all_to_all | solution.py:66
  157.8 23.6 %all-gather.2.cloned.1.call-done = bf16[1024,512]{1,0:T(8,128)(2,1)} async-done(((bf16[64,512]{1,0:T(8,128)(2,1)}), bf16[1024,512]{1,0:T(8,128)(2,1)}) %all-gather.2.cloned.1.call-update) | async-done | bytes 1048592 | tf_op jit(solution)/shard_map/all_gather | solution.py:95
  186.3 4.6 %collective-permute-done.11 = bf16[64,1024]{1,0:T(8,128)(2,1)S(1)} collective-permute-done((bf16[64,1024]{1,0:T(8,128)(2,1)S(1)}, bf16[64,1024]{1,0:T(8,128)(2,1)S(1)}, u32[]{:S(2)}, u32[]{:S(2)}) %collective-permute-start.11) | collective-permute-done | bytes 131104 | tf_op jit(solution)/shard_map/ppermute | solution.py:60
  193.1 12.9 %all_to_all.38 = bf16[16,64,128]{2,1,0:T(8,128)(2,1)S(1)} all-to-all(bf16[16,64,128]{2,1,0:T(8,128)(2,1)S(1)} %concatenate.161), channel_id=1, replica_groups=mesh['tm'=16,'tile'=16] {'tile'}, dimensions={0} | all-to-all | bytes 524288 | tf_op jit(solution)/shard_map/all_to_all | solution.py:66
  208.0 3.4 %copy-done = bf16[1,4,1024,1024]{3,2,1,0:T(8,128)(2,1)S(1)} copy-done((bf16[1,4,1024,1024]{3,2,1,0:T(8,128)(2,1)S(1)}, bf16[1,4,1024,1024]{3,2,1,0:T(8,128)(2,1)}, u32[]{:S(2)}) %copy-start) | copy-done | bytes 8388632
  211.3 2.6 %shard_map.59 = bf16[16,64,256]{2,1,0:T(8,128)(2,1)} custom-call(bf16[64,1024]{1,0:T(8,128)(2,1)S(1)} %fusion.5.sigma_ref, bf16[4,1024,1024]{2,1,0:T(8,128)(2,1)S(1)} %bitcast.74), custom_call_target="tpu_custom_call" | custom-call | flops 536870912 | bytes 8388608 | tf_op jit(solution)/shard_map/pallas_call | solution.py:141
  213.9 3.7 %all-to-all-start.6 = ((bf16[16,64,256]{2,1,0:T(8,128)(2,1)}), bf16[16,64,256]{2,1,0:T(8,128)(2,1)S(1)}, u32[]{:S(2)}, u32[]{:S(2)}) async-start(bf16[16,64,256]{2,1,0:T(8,128)(2,1)} %shard_map.59), calls=%async_computation.6 | async-start | bytes 1048576 | tf_op jit(solution)/shard_map/all_to_all | solution.py:66
  218.5 8.1 %all-to-all-done.6 = bf16[16,64,256]{2,1,0:T(8,128)(2,1)S(1)} async-done(((bf16[16,64,256]{2,1,0:T(8,128)(2,1)}), bf16[16,64,256]{2,1,0:T(8,128)(2,1)S(1)}, u32[]{:S(2)}, u32[]{:S(2)}) %all-to-all-start.6) | async-done | bytes 524320 | tf_op jit(solution)/shard_map/all_to_all | solution.py:66
  226.6 3.4 %copy-done.1 = bf16[1,4,1024,1024]{3,2,1,0:T(8,128)(2,1)S(1)} copy-done((bf16[1,4,1024,1024]{3,2,1,0:T(8,128)(2,1)S(1)}, bf16[1,4,1024,1024]{3,2,1,0:T(8,128)(2,1)}, u32[]{:S(2)}) %copy-start.1) | copy-done | bytes 8388632
  230.0 2.7 %shard_map.60 = f32[4,64,1024]{2,1,0:T(8,128)} custom-call(bf16[1024,256]{1,0:T(8,128)(2,1)S(1)} %bitcast.76, bf16[4,1024,1024]{2,1,0:T(8,128)(2,1)S(1)} %bitcast.75, f32[4,64,1024]{2,1,0:T(8,128)S(1)} %bitcast.77), custom_call_target="tpu_custom_call" | custom-call | flops 536870912 | bytes 8388608 | tf_op jit(solution)/shard_map/pallas_call | solution.py:154
  (136 shorter events, 35.5 us)
Async XLA Ops:
  9.1 4.4 %collective-permute-start = (bf16[64,1536]{1,0:T(8,128)(2,1)S(1)}, bf16[64,1536]{1,0:T(8,128)(2,1)S(1)}, u32[]{:S(2)}, u32[]{:S(2)}) collective-permute-start(bf16[64,1536]{1,0:T(8,128)(2,1)S(1)} %pad_maximum_fusion), channel_id=1, source_target_pairs={{0,16},{1,17},{2,18},{3,19},{4,20},{5,21},{6,22},{7,23},{8,24},{9,... | collective-permute-start | bytes 589832 | tf_op jit(solution)/shard_map/ppermute | solution.py:60
  15.1 25.4 %copy-start.13 = (bf16[1,64,1024]{2,1,0:T(8,128)(2,1)S(1)}, bf16[1,64,1024]{2,1,0:T(8,128)(2,1)}, u32[]{:S(2)}) copy-start(bf16[1,64,1024]{2,1,0:T(8,128)(2,1)} %param.5) | copy-start | bytes 393220
  36.4 4.1 %collective-permute-start.1 = (bf16[1024,512]{1,0:T(8,128)(2,1)S(1)}, bf16[1024,512]{1,0:T(8,128)(2,1)S(1)}, u32[]{:S(2)}, u32[]{:S(2)}) collective-permute-start(bf16[1024,512]{1,0:T(8,128)(2,1)S(1)} %bitcast.93), channel_id=1, source_target_pairs={{0,16},{1,17},{2,18},{3,19},{4,20},{5,21},{6,22},{7,23},{8,24},{9,... | collective-permute-start | bytes 3145736 | tf_op jit(solution)/shard_map/ppermute | solution.py:60
  41.4 3.2 %collective-permute-start.2 = (bf16[64,512]{1,0:T(8,128)(2,1)S(1)}, bf16[64,512]{1,0:T(8,128)(2,1)S(1)}, u32[]{:S(2)}, u32[]{:S(2)}) collective-permute-start(bf16[64,512]{1,0:T(8,128)(2,1)S(1)} %get-tuple-element.26), channel_id=1, source_target_pairs={{16,0},{17,1},{18,2},{19,3},{20,4},{21,5},{22,6},{23,7},{24,8},{25... | collective-permute-start | bytes 196616 | tf_op jit(solution)/shard_map/ppermute | solution.py:60
  67.5 8.9 %collective-permute-start.4 = (bf16[1024,512]{1,0:T(8,128)(2,1)S(1)}, bf16[1024,512]{1,0:T(8,128)(2,1)S(1)}, u32[]{:S(2)}, u32[]{:S(2)}) collective-permute-start(bf16[1024,512]{1,0:T(8,128)(2,1)S(1)} %slice.80), channel_id=1, source_target_pairs={{0,16},{1,17},{2,18},{3,19},{4,20},{5,21},{6,22},{7,23},{8,24},{9,... | collective-permute-start | bytes 3145736 | tf_op jit(solution)/shard_map/ppermute | solution.py:60
  69.8 6.6 %collective-permute-start.3 = (bf16[64,1024]{1,0:T(8,128)(2,1)S(1)}, bf16[64,1024]{1,0:T(8,128)(2,1)S(1)}, u32[]{:S(2)}, u32[]{:S(2)}) collective-permute-start(bf16[64,1024]{1,0:T(8,128)(2,1)S(1)} %maximum_select_fusion), channel_id=1, source_target_pairs={{32,0},{33,1},{34,2},{35,3},{36,4},{37,5},{38,6},{39,7},{40,8},{41... | collective-permute-start | bytes 393224 | tf_op jit(solution)/shard_map/ppermute | solution.py:60
  77.3 4.2 %collective-permute-start.5 = (bf16[64,512]{1,0:T(8,128)(2,1)S(1)}, bf16[64,512]{1,0:T(8,128)(2,1)S(1)}, u32[]{:S(2)}, u32[]{:S(2)}) collective-permute-start(bf16[64,512]{1,0:T(8,128)(2,1)S(1)} %get-tuple-element.28), channel_id=1, source_target_pairs={{16,0},{17,1},{18,2},{19,3},{20,4},{21,5},{22,6},{23,7},{24,8},{25... | collective-permute-start | bytes 196616 | tf_op jit(solution)/shard_map/ppermute | solution.py:60
  104.4 10.3 %collective-permute-start.7 = (bf16[1024,512]{1,0:T(8,128)(2,1)S(1)}, bf16[1024,512]{1,0:T(8,128)(2,1)S(1)}, u32[]{:S(2)}, u32[]{:S(2)}) collective-permute-start(bf16[1024,512]{1,0:T(8,128)(2,1)S(1)} %slice.82), channel_id=1, source_target_pairs={{0,16},{1,17},{2,18},{3,19},{4,20},{5,21},{6,22},{7,23},{8,24},{9,... | collective-permute-start | bytes 3145736 | tf_op jit(solution)/shard_map/ppermute | solution.py:60
  106.6 8.7 %copy-start.14 = (f32[64,512]{1,0:T(8,128)}, f32[64,512]{1,0:T(8,128)S(1)}, u32[]{:S(2)}) copy-start(f32[64,512]{1,0:T(8,128)S(1)} %get-tuple-element.19) | copy-start | bytes 393220
  106.7 8.1 %collective-permute-start.6 = (bf16[64,1024]{1,0:T(8,128)(2,1)S(1)}, bf16[64,1024]{1,0:T(8,128)(2,1)S(1)}, u32[]{:S(2)}, u32[]{:S(2)}) collective-permute-start(bf16[64,1024]{1,0:T(8,128)(2,1)S(1)} %maximum_select_fusion.1), channel_id=1, source_target_pairs={{64,0},{65,1},{66,2},{67,3},{68,4},{69,5},{70,6},{71,7},{72,8},{73... | collective-permute-start | bytes 393224 | tf_op jit(solution)/shard_map/ppermute | solution.py:60
  115.7 5.3 %collective-permute-start.8 = (bf16[64,512]{1,0:T(8,128)(2,1)S(1)}, bf16[64,512]{1,0:T(8,128)(2,1)S(1)}, u32[]{:S(2)}, u32[]{:S(2)}) collective-permute-start(bf16[64,512]{1,0:T(8,128)(2,1)S(1)} %get-tuple-element.30), channel_id=1, source_target_pairs={{16,0},{17,1},{18,2},{19,3},{20,4},{21,5},{22,6},{23,7},{24,8},{25... | collective-permute-start | bytes 196616 | tf_op jit(solution)/shard_map/ppermute | solution.py:60
  123.3 25.1 %all-to-all-start.3 = ((bf16[16,64,640]{2,1,0:T(8,128)(2,1)}), bf16[16,64,640]{2,1,0:T(8,128)(2,1)S(1)}, u32[]{:S(2)}, u32[]{:S(2)}) async-start(bf16[16,64,640]{2,1,0:T(8,128)(2,1)} %maximum_maximum_fusion.2), calls=%async_computation.3 | async-start | bytes 2621440 | tf_op jit(solution)/shard_map/all_to_all | solution.py:66
  127.0 54.4 %all-gather.2.cloned.1.call-start = ((), (), s32[]{:S(2)}) async-start(), calls=%async_computation.7 | async-start | bytes 1114112 | tf_op jit(solution)/shard_map/all_gather | solution.py:95
  148.5 3.6 %collective-permute-start.10 = (bf16[1024,512]{1,0:T(8,128)(2,1)S(1)}, bf16[1024,512]{1,0:T(8,128)(2,1)S(1)}, u32[]{:S(2)}, u32[]{:S(2)}) collective-permute-start(bf16[1024,512]{1,0:T(8,128)(2,1)S(1)} %slice.84), channel_id=1, source_target_pairs={{0,16},{1,17},{2,18},{3,19},{4,20},{5,21},{6,22},{7,23},{8,24},{9,... | collective-permute-start | bytes 3145736 | tf_op jit(solution)/shard_map/ppermute | solution.py:60
  150.6 0.7 collective-permute-start.9
  153.4 29.6 %copy-start.8 = (bf16[1024,512]{1,0:T(8,128)(2,1)S(1)}, bf16[1024,512]{1,0:T(8,128)(2,1)}, u32[]{:S(2)}) copy-start(bf16[1024,512]{1,0:T(8,128)(2,1)} %copy-done.7) | copy-start | bytes 3145732
  154.2 28.4 %all-to-all-start.4 = ((bf16[16,64,128]{2,1,0:T(8,128)(2,1)}), bf16[16,64,128]{2,1,0:T(8,128)(2,1)S(1)}, u32[]{:S(2)}, u32[]{:S(2)}) async-start(bf16[16,64,128]{2,1,0:T(8,128)(2,1)} %concatenate.153), calls=%async_computation.4 | async-start | bytes 524288 | tf_op jit(solution)/shard_map/all_to_all | solution.py:66
  181.4 4.9 %collective-permute-start.12 = (bf16[1024,512]{1,0:T(8,128)(2,1)}, bf16[1024,512]{1,0:T(8,128)(2,1)}, u32[]{:S(2)}, u32[]{:S(2)}) collective-permute-start(bf16[1024,512]{1,0:T(8,128)(2,1)} %all-gather.2.cloned.1.call-done), channel_id=1, source_target_pairs={{0,16},{1,17},{2,18},{3,19},{4,20},{5,21},{6,22},{7,23},{8,24},{9,... | collective-permute-start | bytes 3145736 | tf_op jit(solution)/shard_map/ppermute | solution.py:60
  183.3 9.0 %copy-start.4 = (bf16[1024,512]{1,0:T(8,128)(2,1)S(1)}, bf16[1024,512]{1,0:T(8,128)(2,1)}, u32[]{:S(2)}) copy-start(bf16[1024,512]{1,0:T(8,128)(2,1)} %all-gather.2.cloned.1.call-done) | copy-start | bytes 3145732
  183.4 7.5 %collective-permute-start.11 = (bf16[64,1024]{1,0:T(8,128)(2,1)S(1)}, bf16[64,1024]{1,0:T(8,128)(2,1)S(1)}, u32[]{:S(2)}, u32[]{:S(2)}) collective-permute-start(bf16[64,1024]{1,0:T(8,128)(2,1)S(1)} %fusion.26), channel_id=1, source_target_pairs={{32,16},{33,17},{34,18},{35,19},{36,20},{37,21},{38,22},{39,23},{4... | collective-permute-start | bytes 393224 | tf_op jit(solution)/shard_map/ppermute | solution.py:60
  211.3 6.3 %copy-start.18 = (f32[64,512]{1,0:T(8,128)S(1)}, f32[64,512]{1,0:T(8,128)}, u32[]{:S(2)}) copy-start(f32[64,512]{1,0:T(8,128)} %copy-done.17) | copy-start | bytes 393220
  211.3 6.3 %copy-start.20 = (f32[64,512]{1,0:T(8,128)S(1)}, f32[64,512]{1,0:T(8,128)}, u32[]{:S(2)}) copy-start(f32[64,512]{1,0:T(8,128)} %copy-done.19) | copy-start | bytes 393220
  213.9 12.7 %copy-start.2 = (f32[1,4,64,1024]{3,2,1,0:T(8,128)S(1)}, f32[1,4,64,1024]{3,2,1,0:T(8,128)}, u32[]{:S(2)}) copy-start(f32[1,4,64,1024]{3,2,1,0:T(8,128)} %param.7) | copy-start | bytes 3145732
  213.9 12.7 %all-to-all-start.6 = ((bf16[16,64,256]{2,1,0:T(8,128)(2,1)}), bf16[16,64,256]{2,1,0:T(8,128)(2,1)S(1)}, u32[]{:S(2)}, u32[]{:S(2)}) async-start(bf16[16,64,256]{2,1,0:T(8,128)(2,1)} %shard_map.59), calls=%async_computation.6 | async-start | bytes 1048576 | tf_op jit(solution)/shard_map/all_to_all | solution.py:66
  (18 other events, 40.7 us)
Sparse Core Ops, SparseCore 0:
  130.3 51.0 all-gather.1

commit v2 on v1

v2 whole, which is shorter than its diff:
```python
import jax
import jax.numpy as jnp
from jax import lax
from jax.experimental import pallas as pl
from jax.experimental.pallas import tpu as pltpu
from jax.sharding import PartitionSpec as P

AXES = ("tm", "tile")
BF16 = jnp.bfloat16
F32 = jnp.float32


def dot(left, right, left_dim, right_dim):
    return lax.dot_general(
        left, right, (((left_dim,), (right_dim,)), ((), ())), preferred_element_type=F32
    )


def interior_rows(sigma_ref, maps_ref, out_ref):
    sigma = sigma_ref[...]
    count = maps_ref.shape[0]
    here, rows, width = out_ref.shape
    lane = 2 * width // count
    low = lax.broadcasted_iota(jnp.int32, (rows, lane), 1) < lane // 2
    for j in range(0, count, 2):
        one, two = [
            jnp.dot(sigma, maps_ref[j + i], preferred_element_type=F32) for i in range(2)
        ]
        to = pl.ds(j // 2 * lane, lane)
        for pair in range(here // 2):
            a = one[:, pair * lane : (pair + 1) * lane]
            b = two[:, pair * lane : (pair + 1) * lane]
            even = jnp.where(low, a, pltpu.roll(b, lane // 2, 1))
            odd = jnp.where(low, pltpu.roll(a, lane // 2, 1), b)
            out_ref[2 * pair, :, to] = even.astype(BF16)
            out_ref[2 * pair + 1, :, to] = odd.astype(BF16)


def interior_sums(cols_ref, maps_ref, inv_ref, out_ref):
    count, rows = inv_ref.shape[:2]
    turned = cols_ref[...].T
    for j in range(count):
        out_ref[j] = inv_ref[j] + jnp.dot(
            turned[j * rows : (j + 1) * rows], maps_ref[j], preferred_element_type=F32
        )


def shards(boundary_inv, coupling, interior_map, interior_inv):
    planes = lax.axis_size("tm") // 2
    tiles = lax.axis_size("tile")
    first = lax.axis_index("tm") % 2 == 0
    chunk, order = boundary_inv.shape[1:]
    half = order // 2

    def move(value, route):
        pairs = []
        for z in range(planes):
            for c in range(2):
                to = route(z, c)
                if to is not None and 0 <= to[0] < planes:
                    for t in range(tiles):
                        source, target = 2 * z + c, 2 * to[0] + to[1]
                        pairs.append((source * tiles + t, target * tiles + t))
        return lax.ppermute(value, AXES, pairs)

    def swap_cores(value):
        return move(value, lambda z, c: (z, 1 - c))

    def from_first(value):
        return move(value, lambda z, c: (z, 1) if c == 0 else None)

    def from_second(value):
        return move(value, lambda z, c: (z, 0) if c else None)

    def exchange(pieces):
        return lax.all_to_all(pieces, "tile", 0, 0)

    def gather(value):
        return exchange(jnp.broadcast_to(value, (tiles, *value.shape)))

    def cut(value):
        pairs = value.reshape(chunk, tiles // 2, 2 * chunk).swapaxes(0, 1)
        turned = jnp.roll(pairs, chunk, 2)
        return jnp.stack([pairs, turned], 1).reshape(tiles, chunk, 2 * chunk)

    def times(left, left_dim, halves):
        return jnp.concatenate([dot(left, h, left_dim, 0) for h in halves], 1)

    def fold(w_cols, halves):
        return times(w_cols, 0, halves)[:chunk]

    def turn(value):
        return exchange(cut(value)).reshape(order, 2 * chunk)

    b_rows = boundary_inv[0]
    f_rows = coupling[0]
    maps = interior_map[0]
    count = maps.shape[0]

    given = swap_cores(jnp.concatenate([f_rows, b_rows.astype(BF16)], 1))
    s_rows = given[:, order:]
    q_rows = jnp.where(first, given[:, :order], f_rows)
    f_half = jnp.where(first, f_rows[:, :half], given[:, half:order])
    odd = jnp.where(first, given[:, :half], f_rows[:, half:])

    pieces = gather(jnp.concatenate([f_half, odd], 1)).reshape(order, order)
    f_mine, odd = pieces[:, :half], pieces[:, half:]
    f_halves = (f_mine, from_second(f_mine))
    odd_other = swap_cores(odd)

    w_rows = times(s_rows, 1, f_halves).astype(BF16)
    own = jnp.where(first, 0, half)
    f_mine = (
        dot(odd, lax.dynamic_slice_in_dim(f_mine, own, half, 0), 1, 0)
        + dot(odd_other, lax.dynamic_slice_in_dim(f_mine, half - own, half, 0), 1, 0)
    ).astype(BF16)
    q_half = lax.dynamic_slice_in_dim(f_mine, lax.axis_index("tile") * chunk, chunk, 0)
    q_half = move(q_half, lambda z, c: (z - 1, c))
    other = swap_cores(q_half)
    sigma = b_rows + fold(turn(w_rows), f_halves)

    f_halves = (f_mine, from_second(f_mine))
    s_rows = move(sigma.astype(BF16), lambda z, c: None if c else (z - 1, c))
    q_rows = jnp.concatenate(
        [jnp.where(first, q_half, other), jnp.where(first, other, q_half)], 1
    )
    f_half = dot(q_rows, f_mine, 1, 0).astype(BF16)
    w_rows = times(s_rows, 1, f_halves).astype(BF16)
    pieces = jnp.concatenate(
        [jnp.broadcast_to(f_half, (tiles, chunk, half)), cut(w_rows)], 2
    )
    pieces = exchange(pieces).reshape(order, half + 2 * chunk)
    sigma = sigma + fold(pieces[:, half:], f_halves)

    f_mine = pieces[:, :half]
    f_halves = (f_mine, from_second(f_mine))
    for done in range(planes - 2, 0, -2):
        s_rows = move(
            sigma.astype(BF16),
            lambda z, c: (z - 2, c) if c == 0 and z in (done, done + 1) else None,
        )
        w_rows = times(s_rows, 1, f_halves).astype(BF16)
        sigma = sigma + fold(turn(w_rows), f_halves)

    x_rows = move(
        sigma.astype(BF16), lambda z, c: (z - 1, 1) if c == 0 else None
    )
    odd_halves = (odd_other, odd)
    w_rows = times(x_rows, 1, odd_halves).astype(BF16)
    update = fold(turn(w_rows), odd_halves)
    sigma = jnp.where(first, sigma, b_rows + update)

    low = sigma.astype(BF16)
    params = pltpu.CompilerParams(vmem_limit_bytes=40 * 2**20)
    cost = pl.CostEstimate(
        flops=2 * count * chunk * order * order,
        bytes_accessed=2 * count * order * order,
        transcendentals=0,
    )
    two = count // 2
    map_spec = pl.BlockSpec((two, order, order), lambda n: (n, 0, 0))
    sum_spec = pl.BlockSpec((two, chunk, order), lambda n: (n, 0, 0))
    v_rows = pl.pallas_call(
        interior_rows,
        grid=(2,),
        in_specs=[pl.BlockSpec((chunk, order), lambda n: (0, 0)), map_spec],
        out_specs=pl.BlockSpec((tiles, chunk, two * chunk), lambda n: (0, 0, n)),
        out_shape=jax.ShapeDtypeStruct((tiles, chunk, count * chunk), BF16),
        compiler_params=params,
        cost_estimate=cost,
    )(low, maps)
    v_cols = exchange(v_rows).reshape(order, count * chunk)
    interior_cov = pl.pallas_call(
        interior_sums,
        grid=(2,),
        in_specs=[
            pl.BlockSpec((order, two * chunk), lambda n: (0, n)),
            map_spec,
            sum_spec,
        ],
        out_specs=sum_spec,
        out_shape=jax.ShapeDtypeStruct((count, chunk, order), F32),
        compiler_params=params,
        cost_estimate=cost,
    )(v_cols, maps, interior_inv[0])
    return sigma[None], interior_cov[None]


def solution(mesh):
    in_specs = (
        P("tm", "tile", None),
        P("tm", "tile", None),
        P("tm", None, None, None),
        P("tm", None, "tile", None),
    )
    out_specs = (P("tm", "tile", None), P("tm", None, "tile", None))
    return jax.shard_map(shards, mesh=mesh, in_specs=in_specs, out_specs=out_specs, check_vma=False)
```

time: 243 us -> 209 us (0.86)
  waiting for transfers between devices: 77.5 us -> 39.2 us
  blocking collectives: 78.4 us -> 106 us
  between operations: 14.8 us -> 1.25 us
  local copies, waits for them, and re-layouts: 11.8 us -> 3.36 us
  matrix products: 8.55 us -> 16.4 us
  starting transfers between devices: 36.4 us -> 30.6 us
    all_to_all x4 -> x7, blocking collectives: 78.4 us -> 106 us  [exchange(): return lax.all_to_all(pieces, 'tile', 0, 0)]
    all_to_all x3 -> x1, waiting for transfers between devices: 28.8 us -> 4.78 us  [exchange(): return lax.all_to_all(pieces, 'tile', 0, 0)]
    all_gather x1 -> x0, waiting for transfers between devices: 23.6 us -> none  [shards(): odd_mine = lax.all_gather(odd_half, 'tile', axis=0, tiled=True)]
    ppermute x13 -> x12, waiting for transfers between devices: 24.4 us -> 34.4 us  [move(): return lax.ppermute(value, AXES, pairs)]
    unnamed x50 -> x22, local copies, waits for them, and re-layouts: 8.74 us -> 0.65 us
    dot_general x20 -> x27, matrix products: 8.55 us -> 16.4 us  [dot(): lax.dot_general(left, right, (((left_dim,), (right_dim,)), ((), ())), pre...]
    all_to_all x3 -> x1, starting transfers between devices: 10.9 us -> 4.33 us  [exchange(): return lax.all_to_all(pieces, 'tile', 0, 0)]
    ppermute x13 -> x12, starting transfers between devices: 25.4 us -> 26.3 us  [move(): return lax.ppermute(value, AXES, pairs)]
  transfers between devices with their start and end apart: 17 -> 13, of which waited for: 13 -> 6; matrix products, arithmetic and copies ran while one was open for 2% -> 5% of each run, Pallas kernels for 0% -> 0%
where the time goes in v2:
time: 209 us; the launch traced here: 208 us
  blocking collectives  106 us (51%)
  waiting for transfers between devices  39.2 us (19%)
  starting transfers between devices  30.6 us (15%)
  matrix products  16.4 us (8%)
  other arithmetic  6.34 us (3%)
  Pallas kernels  4.62 us (2%)
  local copies, waits for them, and re-layouts  3.36 us (2%)
    all_to_all x7, blocking collectives, exchange(): return lax.all_to_all(pieces, 'tile', 0, 0)  106 us
    ppermute x12, waiting for transfers between devices, move(): return lax.ppermute(value, AXES, pairs)  34.4 us
    ppermute x12, starting transfers between devices, move(): return lax.ppermute(value, AXES, pairs)  26.3 us
    dot_general x27, matrix products, dot(): lax.dot_general(left, right, (((left_dim,), (right_dim,)), ((), ())), pre...  16.4 us
    all_to_all x1, waiting for transfers between devices, exchange(): return lax.all_to_all(pieces, 'tile', 0, 0)  4.78 us
    all_to_all x1, starting transfers between devices, exchange(): return lax.all_to_all(pieces, 'tile', 0, 0)  4.33 us
  transfers between devices with their start and end apart: 13, of which 6 were waited for; matrix products, arithmetic and copies ran while one was open for 5% of the time, Pallas kernels for 0%

profile of v2, /device:TPU:1, one launch (start us, length us, event | category | flops | bytes accessed | tf_op | source)
XLA Modules:
  0.0 207.8 jit_solution(13009679391192641171)
XLA Ops:
  2.5 3.3 %collective-permute-start = (bf16[64,2048]{1,0:T(8,128)(2,1)S(1)}, bf16[64,2048]{1,0:T(8,128)(2,1)S(1)}, u32[]{:S(2)}, u32[]{:S(2)}) collective-permute-start(bf16[64,2048]{1,0:T(8,128)(2,1)S(1)} %pad_maximum_fusion.7), channel_id=1, source_target_pairs={{0,16},{1,17},{2,18},{3,19},{4,20},{5,21},{6,22},{7,23},{8,24},{9,... | collective-permute-start | bytes 786440 | tf_op jit(solution)/shard_map/ppermute | solution.py:64
  8.2 32.4 %all_to_all.40 = bf16[16,64,1024]{2,1,0:T(8,128)(2,1)S(1)} all-to-all(bf16[16,64,1024]{2,1,0:T(8,128)(2,1)S(1)} %broadcast_in_dim.12), channel_id=1, replica_groups=mesh['tm'=16,'tile'=16] {'tile'}, dimensions={0} | all-to-all | bytes 4194304 | tf_op jit(solution)/shard_map/all_to_all | solution.py:76
  40.6 1.5 fusion.59
  42.0 3.7 %collective-permute-start.1 = (bf16[1024,512]{1,0:T(8,128)(2,1)}, bf16[1024,512]{1,0:T(8,128)(2,1)S(1)}, u32[]{:S(2)}, u32[]{:S(2)}) collective-permute-start(bf16[1024,512]{1,0:T(8,128)(2,1)} %get-tuple-element.9), channel_id=1, source_target_pairs={{16,0},{17,1},{18,2},{19,3},{20,4},{21,5},{22,6},{23,7},{24,8},{25... | collective-permute-start | bytes 3145736 | tf_op jit(solution)/shard_map/ppermute | solution.py:64
  46.2 1.7 fusion.13
  49.7 2.1 %add_convert_fusion = bf16[1024,512]{1,0:T(8,128)(2,1)S(1)} fusion(f32[1024,512]{1,0:T(8,128)S(1)} %fusion.13, bf16[1024,512]{1,0:T(8,128)(2,1)S(1)} %collective-permute-done.2, bf16[1024,512]{1,0:T(8,128)(2,1)} %get-tuple-element.9, s32[]{:T(128)S(6)} %select_n.52), kind=kOutput, calls=%fused_computation | convolution fusion | flops 537919488 | bytes 4718596 | tf_op jit(solution)/shard_map/dot_general | solution.py:14
  51.8 1.3 collective-permute-start.3
  53.3 4.2 %collective-permute-done.3 = bf16[64,512]{1,0:T(8,128)(2,1)S(1)} collective-permute-done((bf16[64,512]{1,0:T(8,128)(2,1)S(1)}, bf16[64,512]{1,0:T(8,128)(2,1)S(1)}, u32[]{:S(2)}, u32[]{:S(2)}) %collective-permute-start.3) | collective-permute-done | bytes 65568 | tf_op jit(solution)/shard_map/ppermute | solution.py:64
  59.2 4.3 %all-to-all-start.1 = ((bf16[16,64,128]{2,1,0:T(8,128)(2,1)}), bf16[16,64,128]{2,1,0:T(8,128)(2,1)}, u32[]{:S(2)}, u32[]{:S(2)}) async-start(bf16[16,64,128]{2,1,0:T(8,128)(2,1)} %bitcast.197), calls=%async_computation.1 | async-start | bytes 524288 | tf_op jit(solution)/shard_map/all_to_all | solution.py:76
  63.5 2.9 %collective-permute-start.6 = (bf16[1024,512]{1,0:T(8,128)(2,1)S(1)}, bf16[1024,512]{1,0:T(8,128)(2,1)}, u32[]{:S(2)}, u32[]{:S(2)}) collective-permute-start(bf16[1024,512]{1,0:T(8,128)(2,1)S(1)} %add_convert_fusion), channel_id=1, source_target_pairs={{16,0},{17,1},{18,2},{19,3},{20,4},{21,5},{22,6},{23,7},{24,8},{25... | collective-permute-start | bytes 3145736 | tf_op jit(solution)/shard_map/ppermute | solution.py:64
  67.3 4.8 %all-to-all-done.1 = bf16[16,64,128]{2,1,0:T(8,128)(2,1)} async-done(((bf16[16,64,128]{2,1,0:T(8,128)(2,1)}), bf16[16,64,128]{2,1,0:T(8,128)(2,1)}, u32[]{:S(2)}, u32[]{:S(2)}) %all-to-all-start.1) | async-done | bytes 262176 | tf_op jit(solution)/shard_map/all_to_all | solution.py:76
  73.3 1.6 fusion.66
  76.4 1.5 fusion.3
  78.4 16.2 %all_to_all.41 = bf16[16,64,640]{2,1,0:T(8,128)(2,1)S(1)} all-to-all(bf16[16,64,640]{2,1,0:T(8,128)(2,1)S(1)} %pad_maximum_fusion), channel_id=1, replica_groups=mesh['tm'=16,'tile'=16] {'tile'}, dimensions={0} | all-to-all | bytes 2621440 | tf_op jit(solution)/shard_map/all_to_all | solution.py:76
  94.7 10.0 %collective-permute-start.8 = (bf16[1024,512]{1,0:T(8,128)(2,1)S(1)}, bf16[1024,512]{1,0:T(8,128)(2,1)S(1)}, u32[]{:S(2)}, u32[]{:S(2)}) collective-permute-start(bf16[1024,512]{1,0:T(8,128)(2,1)S(1)} %slice.122), channel_id=1, source_target_pairs={{16,0},{17,1},{18,2},{19,3},{20,4},{21,5},{22,6},{23,7},{24,8},{25... | collective-permute-start | bytes 3145736 | tf_op jit(solution)/shard_map/ppermute | solution.py:64
  105.0 1.6 fusion.22
  108.3 11.2 %all_to_all.42 = bf16[16,64,128]{2,1,0:T(8,128)(2,1)S(1)} all-to-all(bf16[16,64,128]{2,1,0:T(8,128)(2,1)S(1)} %bitcast.198), channel_id=1, replica_groups=mesh['tm'=16,'tile'=16] {'tile'}, dimensions={0} | all-to-all | bytes 524288 | tf_op jit(solution)/shard_map/all_to_all | solution.py:76
  121.8 10.4 %all_to_all.43 = bf16[16,64,128]{2,1,0:T(8,128)(2,1)S(1)} all-to-all(bf16[16,64,128]{2,1,0:T(8,128)(2,1)S(1)} %bitcast.199), channel_id=1, replica_groups=mesh['tm'=16,'tile'=16] {'tile'}, dimensions={0} | all-to-all | bytes 524288 | tf_op jit(solution)/shard_map/all_to_all | solution.py:76
  134.6 10.5 %all_to_all.44 = bf16[16,64,128]{2,1,0:T(8,128)(2,1)S(1)} all-to-all(bf16[16,64,128]{2,1,0:T(8,128)(2,1)S(1)} %bitcast.200), channel_id=1, replica_groups=mesh['tm'=16,'tile'=16] {'tile'}, dimensions={0} | all-to-all | bytes 524288 | tf_op jit(solution)/shard_map/all_to_all | solution.py:76
  147.2 28.3 %collective-permute-done.11 = bf16[64,1024]{1,0:T(8,128)(2,1)S(1)} collective-permute-done((bf16[64,1024]{1,0:T(8,128)(2,1)S(1)}, bf16[64,1024]{1,0:T(8,128)(2,1)S(1)}, u32[]{:S(2)}, u32[]{:S(2)}) %collective-permute-start.11) | collective-permute-done | bytes 131104 | tf_op jit(solution)/shard_map/ppermute | solution.py:64
  176.4 10.3 %all_to_all.45 = bf16[16,64,128]{2,1,0:T(8,128)(2,1)S(1)} all-to-all(bf16[16,64,128]{2,1,0:T(8,128)(2,1)S(1)} %bitcast.201), channel_id=1, replica_groups=mesh['tm'=16,'tile'=16] {'tile'}, dimensions={0} | all-to-all | bytes 524288 | tf_op jit(solution)/shard_map/all_to_all | solution.py:76
  188.2 2.0 shard_map.59
  190.2 14.9 %all_to_all.46 = bf16[16,64,256]{2,1,0:T(8,128)(2,1)S(1)} all-to-all(bf16[16,64,256]{2,1,0:T(8,128)(2,1)S(1)} %shard_map.59), channel_id=1, replica_groups=mesh['tm'=16,'tile'=16] {'tile'}, dimensions={0} | all-to-all | bytes 1048576 | tf_op jit(solution)/shard_map/all_to_all | solution.py:76
  205.1 2.7 %shard_map.60 = f32[4,64,1024]{2,1,0:T(8,128)} custom-call(bf16[1024,256]{1,0:T(8,128)(2,1)S(1)} %bitcast.159, bf16[4,1024,1024]{2,1,0:T(8,128)(2,1)S(1)} %bitcast.158, f32[4,64,1024]{2,1,0:T(8,128)S(1)} %bitcast.160), custom_call_target="tpu_custom_call" | custom-call | flops 536870912 | bytes 8388608 | tf_op jit(solution)/shard_map/pallas_call | solution.py:173
  (102 shorter events, 23.0 us)
Async XLA Ops:
  2.5 4.5 %collective-permute-start = (bf16[64,2048]{1,0:T(8,128)(2,1)S(1)}, bf16[64,2048]{1,0:T(8,128)(2,1)S(1)}, u32[]{:S(2)}, u32[]{:S(2)}) collective-permute-start(bf16[64,2048]{1,0:T(8,128)(2,1)S(1)} %pad_maximum_fusion.7), channel_id=1, source_target_pairs={{0,16},{1,17},{2,18},{3,19},{4,20},{5,21},{6,22},{7,23},{8,24},{9,... | collective-permute-start | bytes 786440 | tf_op jit(solution)/shard_map/ppermute | solution.py:64
  42.0 6.2 %collective-permute-start.1 = (bf16[1024,512]{1,0:T(8,128)(2,1)}, bf16[1024,512]{1,0:T(8,128)(2,1)S(1)}, u32[]{:S(2)}, u32[]{:S(2)}) collective-permute-start(bf16[1024,512]{1,0:T(8,128)(2,1)} %get-tuple-element.9), channel_id=1, source_target_pairs={{16,0},{17,1},{18,2},{19,3},{20,4},{21,5},{22,6},{23,7},{24,8},{25... | collective-permute-start | bytes 3145736 | tf_op jit(solution)/shard_map/ppermute | solution.py:64
  45.8 3.9 %collective-permute-start.2 = (bf16[1024,512]{1,0:T(8,128)(2,1)}, bf16[1024,512]{1,0:T(8,128)(2,1)S(1)}, u32[]{:S(2)}, u32[]{:S(2)}) collective-permute-start(bf16[1024,512]{1,0:T(8,128)(2,1)} %get-tuple-element.8), channel_id=1, source_target_pairs={{0,16},{1,17},{2,18},{3,19},{4,20},{5,21},{6,22},{7,23},{8,24},{9,... | collective-permute-start | bytes 3145736 | tf_op jit(solution)/shard_map/ppermute | solution.py:64
  48.2 1.0 copy-start.3
  49.7 2.1 %copy-start.1 = (bf16[1024,512]{1,0:T(8,128)(2,1)}, bf16[1024,512]{1,0:T(8,128)(2,1)S(1)}, u32[]{:S(2)}) copy-start(bf16[1024,512]{1,0:T(8,128)(2,1)S(1)} %collective-permute-done.2) | copy-start | bytes 3145732
  51.8 5.6 %collective-permute-start.3 = (bf16[64,512]{1,0:T(8,128)(2,1)S(1)}, bf16[64,512]{1,0:T(8,128)(2,1)S(1)}, u32[]{:S(2)}, u32[]{:S(2)}) collective-permute-start(bf16[64,512]{1,0:T(8,128)(2,1)S(1)} %constant_dynamic-slice_fusion), channel_id=1, source_target_pairs={{32,0},{33,1},{34,2},{35,3},{36,4},{37,5},{38,6},{39,7},{40,8},{41... | collective-permute-start | bytes 196616 | tf_op jit(solution)/shard_map/ppermute | solution.py:64
  57.4 9.0 %copy-start.5 = (bf16[64,512]{1,0:T(8,128)(2,1)}, bf16[64,512]{1,0:T(8,128)(2,1)S(1)}, u32[]{:S(2)}) copy-start(bf16[64,512]{1,0:T(8,128)(2,1)S(1)} %collective-permute-done.3) | copy-start | bytes 196612
  57.4 9.0 %collective-permute-start.4 = (bf16[64,512]{1,0:T(8,128)(2,1)S(1)}, bf16[64,512]{1,0:T(8,128)(2,1)}, u32[]{:S(2)}, u32[]{:S(2)}) collective-permute-start(bf16[64,512]{1,0:T(8,128)(2,1)S(1)} %collective-permute-done.3), channel_id=1, source_target_pairs={{0,16},{1,17},{2,18},{3,19},{4,20},{5,21},{6,22},{7,23},{8,24},{9,... | collective-permute-start | bytes 196616 | tf_op jit(solution)/shard_map/ppermute | solution.py:64
  59.2 15.8 %copy-start.4 = (f32[1,64,1024]{2,1,0:T(8,128)S(1)}, f32[1,64,1024]{2,1,0:T(8,128)}, u32[]{:S(2)}) copy-start(f32[1,64,1024]{2,1,0:T(8,128)} %param.4) | copy-start | bytes 786436
  59.2 12.9 %all-to-all-start.1 = ((bf16[16,64,128]{2,1,0:T(8,128)(2,1)}), bf16[16,64,128]{2,1,0:T(8,128)(2,1)}, u32[]{:S(2)}, u32[]{:S(2)}) async-start(bf16[16,64,128]{2,1,0:T(8,128)(2,1)} %bitcast.197), calls=%async_computation.1 | async-start | bytes 524288 | tf_op jit(solution)/shard_map/all_to_all | solution.py:76
  63.5 12.9 %collective-permute-start.6 = (bf16[1024,512]{1,0:T(8,128)(2,1)S(1)}, bf16[1024,512]{1,0:T(8,128)(2,1)}, u32[]{:S(2)}, u32[]{:S(2)}) collective-permute-start(bf16[1024,512]{1,0:T(8,128)(2,1)S(1)} %add_convert_fusion), channel_id=1, source_target_pairs={{16,0},{17,1},{18,2},{19,3},{20,4},{21,5},{22,6},{23,7},{24,8},{25... | collective-permute-start | bytes 3145736 | tf_op jit(solution)/shard_map/ppermute | solution.py:64
  75.0 1.0 collective-permute-start.5
  94.7 13.0 %collective-permute-start.8 = (bf16[1024,512]{1,0:T(8,128)(2,1)S(1)}, bf16[1024,512]{1,0:T(8,128)(2,1)S(1)}, u32[]{:S(2)}, u32[]{:S(2)}) collective-permute-start(bf16[1024,512]{1,0:T(8,128)(2,1)S(1)} %slice.122), channel_id=1, source_target_pairs={{16,0},{17,1},{18,2},{19,3},{20,4},{21,5},{22,6},{23,7},{24,8},{25... | collective-permute-start | bytes 3145736 | tf_op jit(solution)/shard_map/ppermute | solution.py:64
  106.7 0.7 collective-permute-start.7
  120.2 0.7 collective-permute-start.9
  133.0 0.7 collective-permute-start.10
  134.3 53.9 %slice-start = ((s8[8388608]{0:T(1024)(128)(4,1)}), s8[4194304]{0:T(1024)(128)(4,1)S(1)}, s32[]{:S(2)}) async-start(s8[8388608]{0:T(1024)(128)(4,1)} %bitcast.155), calls=%async_computation.8 | async-start | bytes 8388608
  145.1 30.3 %copy-start.2 = (bf16[1024,512]{1,0:T(8,128)(2,1)S(1)}, bf16[1024,512]{1,0:T(8,128)(2,1)}, u32[]{:S(2)}) copy-start(bf16[1024,512]{1,0:T(8,128)(2,1)} %copy-done.1) | copy-start | bytes 3145732
  145.9 29.6 %collective-permute-start.11 = (bf16[64,1024]{1,0:T(8,128)(2,1)S(1)}, bf16[64,1024]{1,0:T(8,128)(2,1)S(1)}, u32[]{:S(2)}, u32[]{:S(2)}) collective-permute-start(bf16[64,1024]{1,0:T(8,128)(2,1)S(1)} %fusion.36), channel_id=1, source_target_pairs={{32,16},{33,17},{34,18},{35,19},{36,20},{37,21},{38,22},{39,23},{4... | collective-permute-start | bytes 393224 | tf_op jit(solution)/shard_map/ppermute | solution.py:64
  175.8 12.4 %slice-start.1 = ((s8[8388608]{0:T(1024)(128)(4,1)}), s8[4194304]{0:T(1024)(128)(4,1)S(1)}, s32[]{:S(2)}) async-start(s8[8388608]{0:T(1024)(128)(4,1)} %bitcast.155), calls=%async_computation.9 | async-start | bytes 8388608
  188.2 16.9 %copy-start = (f32[1,4,64,1024]{3,2,1,0:T(8,128)S(1)}, f32[1,4,64,1024]{3,2,1,0:T(8,128)}, u32[]{:S(2)}) copy-start(f32[1,4,64,1024]{3,2,1,0:T(8,128)} %param.7) | copy-start | bytes 3145732

commit v3 on v2

--- a/solution.py
+++ b/solution.py
@@ -1,3 +1,5 @@
+import functools
+
 import jax
 import jax.numpy as jnp
 from jax import lax
@@ -14,6 +16,32 @@
     return lax.dot_general(
         left, right, (((left_dim,), (right_dim,)), ((), ())), preferred_element_type=F32
     )
+
+
+def spread_rows(rows_ref, out_ref):
+    for t in range(out_ref.shape[0]):
+        out_ref[t] = rows_ref[...]
+
+
+def spread_products(with_rows, s_ref, rows_ref, mine_ref, other_ref, out_ref):
+    tiles, rows, width = out_ref.shape
+    lane = 2 * rows
+    start = width - lane
+    if with_rows is not None:
+        all_rows = rows_ref[...]
+        if with_rows:
+            all_rows = jnp.dot(all_rows, mine_ref[...], preferred_element_type=F32)
+            all_rows = all_rows.astype(BF16)
+        for t in range(tiles):
+            out_ref[t, :, :start] = all_rows
+    t = 0
+    for ref in (mine_ref, other_ref):
+        product = jnp.dot(s_ref[...], ref[...], preferred_element_type=F32)
+        for at in range(0, product.shape[1], lane):
+            pair = product[:, at : at + lane]
+            out_ref[t, :, start:] = pair.astype(BF16)
+            out_ref[t + 1, :, start:] = pltpu.roll(pair, rows, 1).astype(BF16)
+            t += 2
 
 
 def interior_rows(sigma_ref, maps_ref, out_ref):
@@ -76,12 +104,14 @@
         return lax.all_to_all(pieces, "tile", 0, 0)
 
     def gather(value):
-        return exchange(jnp.broadcast_to(value, (tiles, *value.shape)))
-
-    def cut(value):
-        pairs = value.reshape(chunk, tiles // 2, 2 * chunk).swapaxes(0, 1)
-        turned = jnp.roll(pairs, chunk, 2)
-        return jnp.stack([pairs, turned], 1).reshape(tiles, chunk, 2 * chunk)
+        return exchange(placed(spread_rows, value.shape[1])(value))
+
+    def placed(kernel, width):
+        return pl.pallas_call(
+            kernel,
+            out_shape=pltpu.VMEM((tiles, chunk, width), BF16),
+            compiler_params=pltpu.CompilerParams(vmem_limit_bytes=12 * 2**20),
+        )
 
     def times(left, left_dim, halves):
         return jnp.concatenate([dot(left, h, left_dim, 0) for h in halves], 1)
@@ -89,8 +119,17 @@
     def fold(w_cols, halves):
         return times(w_cols, 0, halves)[:chunk]
 
-    def turn(value):
-        return exchange(cut(value)).reshape(order, 2 * chunk)
+    def turn(s_rows, f_halves):
+        pieces = placed(functools.partial(spread_products, None), 2 * chunk)(
+            s_rows, s_rows, *f_halves
+        )
+        return exchange(pieces).reshape(order, 2 * chunk)
+
+    def share(with_rows, s_rows, rows, f_halves):
+        pieces = placed(functools.partial(spread_products, with_rows), half + 2 * chunk)(
+            s_rows, rows, *f_halves
+        )
+        return pieces
 
     b_rows = boundary_inv[0]
     f_rows = coupling[0]
@@ -103,55 +142,56 @@
     f_half = jnp.where(first, f_rows[:, :half], given[:, half:order])
     odd = jnp.where(first, given[:, :half], f_rows[:, half:])
 
-    pieces = gather(jnp.concatenate([f_half, odd], 1)).reshape(order, order)
-    f_mine, odd = pieces[:, :half], pieces[:, half:]
+    def after(value, anchor):
+        return lax.optimization_barrier((value, anchor))[0]
+
+    f_mine = gather(f_half).reshape(order, half)
     f_halves = (f_mine, from_second(f_mine))
+
+    q_half = dot(q_rows, f_mine, 1, 0).astype(BF16)
+    q_half = move(q_half, lambda z, c: (z - 1, c))
+    pieces = share(False, s_rows, odd, f_halves)
+    pieces, q_half = lax.optimization_barrier((pieces, q_half))
+    other = swap_cores(q_half)
+    pieces = exchange(pieces).reshape(order, half + 2 * chunk)
+    odd = pieces[:, :half]
     odd_other = swap_cores(odd)
-
-    w_rows = times(s_rows, 1, f_halves).astype(BF16)
+    sigma = b_rows + fold(pieces[:, half:], f_halves)
+    low = sigma.astype(BF16)
+
     own = jnp.where(first, 0, half)
-    f_mine = (
-        dot(odd, lax.dynamic_slice_in_dim(f_mine, own, half, 0), 1, 0)
-        + dot(odd_other, lax.dynamic_slice_in_dim(f_mine, half - own, half, 0), 1, 0)
-    ).astype(BF16)
-    q_half = lax.dynamic_slice_in_dim(f_mine, lax.axis_index("tile") * chunk, chunk, 0)
-    q_half = move(q_half, lambda z, c: (z - 1, c))
-    other = swap_cores(q_half)
-    sigma = b_rows + fold(turn(w_rows), f_halves)
-
-    f_halves = (f_mine, from_second(f_mine))
-    s_rows = move(sigma.astype(BF16), lambda z, c: None if c else (z - 1, c))
+    f_halves = [
+        dot(odd, lax.dynamic_slice_in_dim(f, own, half, 0), 1, 0)
+        + dot(odd_other, lax.dynamic_slice_in_dim(f, half - own, half, 0), 1, 0)
+        for f in after(f_halves, low)
+    ]
+    f_halves = [f.astype(BF16) for f in f_halves]
+    s_rows = move(low, lambda z, c: None if c else (z - 1, c))
     q_rows = jnp.concatenate(
         [jnp.where(first, q_half, other), jnp.where(first, other, q_half)], 1
     )
-    f_half = dot(q_rows, f_mine, 1, 0).astype(BF16)
-    w_rows = times(s_rows, 1, f_halves).astype(BF16)
-    pieces = jnp.concatenate(
-        [jnp.broadcast_to(f_half, (tiles, chunk, half)), cut(w_rows)], 2
-    )
+    pieces = share(True, s_rows, q_rows, f_halves)
     pieces = exchange(pieces).reshape(order, half + 2 * chunk)
     sigma = sigma + fold(pieces[:, half:], f_halves)
-
-    f_mine = pieces[:, :half]
+    low = sigma.astype(BF16)
+    f_mine = after(pieces[:, :half], low)
     f_halves = (f_mine, from_second(f_mine))
+
     for done in range(planes - 2, 0, -2):
         s_rows = move(
-            sigma.astype(BF16),
+            low,
             lambda z, c: (z - 2, c) if c == 0 and z in (done, done + 1) else None,
         )
-        w_rows = times(s_rows, 1, f_halves).astype(BF16)
-        sigma = sigma + fold(turn(w_rows), f_halves)
-
-    x_rows = move(
-        sigma.astype(BF16), lambda z, c: (z - 1, 1) if c == 0 else None
-    )
+        sigma = sigma + fold(turn(s_rows, f_halves), f_halves)
+        low = sigma.astype(BF16)
+
+    x_rows = move(low, lambda z, c: (z - 1, 1) if c == 0 else None)
     odd_halves = (odd_other, odd)
-    w_rows = times(x_rows, 1, odd_halves).astype(BF16)
-    update = fold(turn(w_rows), odd_halves)
+    update = fold(turn(x_rows, odd_halves), odd_halves)
     sigma = jnp.where(first, sigma, b_rows + update)
 
     low = sigma.astype(BF16)
-    params = pltpu.CompilerParams(vmem_limit_bytes=40 * 2**20)
+    params = pltpu.CompilerParams(vmem_limit_bytes=20 * 2**20)
     cost = pl.CostEstimate(
         flops=2 * count * chunk * order * order,
         bytes_accessed=2 * count * order * order,

time: 209 us -> 198 us (0.947)
  waiting for transfers between devices: 39.2 us -> 54.8 us
  matrix products: 16.4 us -> 7.17 us
  blocking collectives: 106 us -> 97.4 us
  starting transfers between devices: 30.6 us -> 23.9 us
  Pallas kernels: 4.62 us -> 9.27 us
  local copies, waits for them, and re-layouts: 3.36 us -> 0.46 us
  other arithmetic: 6.34 us -> 3.82 us
    all_to_all x1, waiting for transfers between devices: 4.78 us -> 20.9 us  [exchange(): return lax.all_to_all(pieces, 'tile', 0, 0)]
    dot_general x27 -> x17, matrix products: 16.4 us -> 7.17 us  [dot(): lax.dot_general(left, right, (((left_dim,), (right_dim,)), ((), ())), pre...]
    all_to_all x7, blocking collectives: 106 us -> 97.4 us  [exchange(): return lax.all_to_all(pieces, 'tile', 0, 0)]
    ppermute x12 -> x11, starting transfers between devices: 26.3 us -> 20.2 us  [move(): return lax.ppermute(value, AXES, pairs)]
    pallas_call x0 -> x7, Pallas kernels: none -> 4.67 us  [the longest x2 2.42 us: share(): placed(functools.partial(spread_products, with_rows), half + 2 * chunk)]
    ppermute x12 -> x11, waiting for transfers between devices: 34.4 us -> 33.9 us  [move(): return lax.ppermute(value, AXES, pairs)]
  transfers between devices with their start and end apart: 13 -> 12, of which waited for: 6 -> 7; matrix products, arithmetic and copies ran while one was open for 5% -> 2% of each run, Pallas kernels for 0% -> 1%
where the time goes in v3:
time: 198 us
  blocking collectives  97.4 us (49%)
  waiting for transfers between devices  54.8 us (28%)
  starting transfers between devices  23.9 us (12%)
  Pallas kernels  9.27 us (5%)
  matrix products  7.17 us (4%)
  other arithmetic  3.82 us (2%)
    all_to_all x7, blocking collectives, exchange(): return lax.all_to_all(pieces, 'tile', 0, 0)  97.4 us
    ppermute x11, waiting for transfers between devices, move(): return lax.ppermute(value, AXES, pairs)  33.9 us
    all_to_all x1, waiting for transfers between devices, exchange(): return lax.all_to_all(pieces, 'tile', 0, 0)  20.9 us
    ppermute x11, starting transfers between devices, move(): return lax.ppermute(value, AXES, pairs)  20.2 us
    dot_general x17, matrix products, dot(): lax.dot_general(left, right, (((left_dim,), (right_dim,)), ((), ())), pre...  7.17 us
  transfers between devices with their start and end apart: 12, of which 7 were waited for; matrix products, arithmetic and copies ran while one was open for 2% of the time, Pallas kernels for 1%

profile of v3, /device:TPU:1, one launch (start us, length us, event | category | flops | bytes accessed | tf_op | source)
XLA Modules:
  0.0 197.8 jit_solution(6665615662080120014)
XLA Ops:
  0.6 1.0 bitcast_convert_fusion
  1.6 0.9 pad_maximum_fusion.6
  2.5 3.3 %collective-permute-start = (bf16[64,2048]{1,0:T(8,128)(2,1)S(1)}, bf16[64,2048]{1,0:T(8,128)(2,1)S(1)}, u32[]{:S(2)}, u32[]{:S(2)}) collective-permute-start(bf16[64,2048]{1,0:T(8,128)(2,1)S(1)} %pad_maximum_fusion.6), channel_id=1, source_target_pairs={{0,16},{1,17},{2,18},{3,19},{4,20},{5,21},{6,22},{7,23},{8,24},{9,... | collective-permute-start | bytes 786440 | tf_op jit(solution)/shard_map/ppermute | solution.py:92
  5.9 1.2 collective-permute-done
  8.0 21.3 %all_to_all.40 = bf16[16,64,512]{2,1,0:T(8,128)(2,1)S(1)} all-to-all(bf16[16,64,512]{2,1,0:T(8,128)(2,1)S(1)} %shard_map.59), channel_id=1, replica_groups=mesh['tm'=16,'tile'=16] {'tile'}, dimensions={0} | all-to-all | bytes 2097152 | tf_op jit(solution)/shard_map/all_to_all | solution.py:104
  29.3 3.7 %collective-permute-start.1 = (bf16[1024,512]{1,0:T(8,128)(2,1)S(1)}, bf16[1024,512]{1,0:T(8,128)(2,1)S(1)}, u32[]{:S(2)}, u32[]{:S(2)}) collective-permute-start(bf16[1024,512]{1,0:T(8,128)(2,1)S(1)} %bitcast.53), channel_id=1, source_target_pairs={{16,0},{17,1},{18,2},{19,3},{20,4},{21,5},{22,6},{23,7},{24,8},{25... | collective-permute-start | bytes 3145736 | tf_op jit(solution)/shard_map/ppermute | solution.py:92
  33.3 1.3 collective-permute-start.2
  35.2 1.6 shard_map.60
  36.8 2.0 %collective-permute-done.2 = bf16[64,512]{1,0:T(8,128)(2,1)S(1)} collective-permute-done((bf16[64,512]{1,0:T(8,128)(2,1)S(1)}, bf16[64,512]{1,0:T(8,128)(2,1)S(1)}, u32[]{:S(2)}, u32[]{:S(2)}) %collective-permute-start.2) | collective-permute-done | bytes 65568 | tf_op jit(solution)/shard_map/ppermute | solution.py:92
  38.8 3.7 %all-to-all-start.1 = ((bf16[16,64,640]{2,1,0:T(8,128)(2,1)}), bf16[16,64,640]{2,1,0:T(8,128)(2,1)S(1)}, u32[]{:S(2)}, u32[]{:S(2)}) async-start(bf16[16,64,640]{2,1,0:T(8,128)(2,1)} %shard_map.60), calls=%async_computation.1 | async-start | bytes 2621440 | tf_op jit(solution)/shard_map/all_to_all | solution.py:104
  43.0 20.9 %all-to-all-done.1 = bf16[16,64,640]{2,1,0:T(8,128)(2,1)S(1)} async-done(((bf16[16,64,640]{2,1,0:T(8,128)(2,1)}), bf16[16,64,640]{2,1,0:T(8,128)(2,1)S(1)}, u32[]{:S(2)}, u32[]{:S(2)}) %all-to-all-start.1) | async-done | bytes 1310752 | tf_op jit(solution)/shard_map/all_to_all | solution.py:104
  64.0 1.3 collective-permute-start.5
  71.2 19.7 %all_to_all.41 = bf16[16,64,640]{2,1,0:T(8,128)(2,1)S(1)} all-to-all(bf16[16,64,640]{2,1,0:T(8,128)(2,1)S(1)} %shard_map.61), channel_id=1, replica_groups=mesh['tm'=16,'tile'=16] {'tile'}, dimensions={0} | all-to-all | bytes 2621440 | tf_op jit(solution)/shard_map/all_to_all | solution.py:104
  91.8 5.8 %collective-permute-start.7 = (bf16[1024,512]{1,0:T(8,128)(2,1)S(1)}, bf16[1024,512]{1,0:T(8,128)(2,1)S(1)}, u32[]{:S(2)}, u32[]{:S(2)}) collective-permute-start(bf16[1024,512]{1,0:T(8,128)(2,1)S(1)} %slice.73.mine_ref), channel_id=1, source_target_pairs={{16,0},{17,1},{18,2},{19,3},{20,4},{21,5},{22,6},{23,7},{24,8},{25... | collective-permute-start | bytes 3145736 | tf_op jit(solution)/shard_map/ppermute | solution.py:92
  98.3 1.5 collective-permute-done.7.other_ref
  100.4 10.7 %all_to_all.42 = bf16[16,64,128]{2,1,0:T(8,128)(2,1)S(1)} all-to-all(bf16[16,64,128]{2,1,0:T(8,128)(2,1)S(1)} %shard_map.62), channel_id=1, replica_groups=mesh['tm'=16,'tile'=16] {'tile'}, dimensions={0} | all-to-all | bytes 524288 | tf_op jit(solution)/shard_map/all_to_all | solution.py:104
  113.1 10.2 %all_to_all.43 = bf16[16,64,128]{2,1,0:T(8,128)(2,1)S(1)} all-to-all(bf16[16,64,128]{2,1,0:T(8,128)(2,1)S(1)} %shard_map.63), channel_id=1, replica_groups=mesh['tm'=16,'tile'=16] {'tile'}, dimensions={0} | all-to-all | bytes 524288 | tf_op jit(solution)/shard_map/all_to_all | solution.py:104
  125.3 10.5 %all_to_all.44 = bf16[16,64,128]{2,1,0:T(8,128)(2,1)S(1)} all-to-all(bf16[16,64,128]{2,1,0:T(8,128)(2,1)S(1)} %shard_map.64), channel_id=1, replica_groups=mesh['tm'=16,'tile'=16] {'tile'}, dimensions={0} | all-to-all | bytes 524288 | tf_op jit(solution)/shard_map/all_to_all | solution.py:104
  136.6 1.6 collective-permute-start.10
  138.1 28.1 %collective-permute-done.10.s_ref.rows_ref = bf16[64,1024]{1,0:T(8,128)(2,1)S(1)} collective-permute-done((bf16[64,1024]{1,0:T(8,128)(2,1)S(1)}, bf16[64,1024]{1,0:T(8,128)(2,1)S(1)}, u32[]{:S(2)}, u32[]{:S(2)}) %collective-permute-start.10) | collective-permute-done | bytes 131104 | tf_op jit(solution)/shard_map/ppermute | solution.py:92
  166.8 10.2 %all_to_all.45 = bf16[16,64,128]{2,1,0:T(8,128)(2,1)S(1)} all-to-all(bf16[16,64,128]{2,1,0:T(8,128)(2,1)S(1)} %shard_map.65), channel_id=1, replica_groups=mesh['tm'=16,'tile'=16] {'tile'}, dimensions={0} | all-to-all | bytes 524288 | tf_op jit(solution)/shard_map/all_to_all | solution.py:104
  178.4 1.9 shard_map.66
  180.4 14.7 %all_to_all.46 = bf16[16,64,256]{2,1,0:T(8,128)(2,1)S(1)} all-to-all(bf16[16,64,256]{2,1,0:T(8,128)(2,1)S(1)} %shard_map.66), channel_id=1, replica_groups=mesh['tm'=16,'tile'=16] {'tile'}, dimensions={0} | all-to-all | bytes 1048576 | tf_op jit(solution)/shard_map/all_to_all | solution.py:104
  195.1 2.7 %shard_map.67 = f32[4,64,1024]{2,1,0:T(8,128)} custom-call(bf16[1024,256]{1,0:T(8,128)(2,1)S(1)} %bitcast.59, bf16[4,1024,1024]{2,1,0:T(8,128)(2,1)S(1)} %bitcast.52, f32[4,64,1024]{2,1,0:T(8,128)S(1)} %bitcast.60), custom_call_target="tpu_custom_call" | custom-call | flops 536870912 | bytes 8388608 | tf_op jit(solution)/shard_map/pallas_call | solution.py:213
  (58 shorter events, 16.9 us)
Async XLA Ops:
  2.5 4.5 %collective-permute-start = (bf16[64,2048]{1,0:T(8,128)(2,1)S(1)}, bf16[64,2048]{1,0:T(8,128)(2,1)S(1)}, u32[]{:S(2)}, u32[]{:S(2)}) collective-permute-start(bf16[64,2048]{1,0:T(8,128)(2,1)S(1)} %pad_maximum_fusion.6), channel_id=1, source_target_pairs={{0,16},{1,17},{2,18},{3,19},{4,20},{5,21},{6,22},{7,23},{8,24},{9,... | collective-permute-start | bytes 786440 | tf_op jit(solution)/shard_map/ppermute | solution.py:92
  8.0 25.0 %copy-start.2 = (bf16[1,64,1024]{2,1,0:T(8,128)(2,1)S(1)}, bf16[1,64,1024]{2,1,0:T(8,128)(2,1)}, u32[]{:S(2)}) copy-start(bf16[1,64,1024]{2,1,0:T(8,128)(2,1)} %param.5) | copy-start | bytes 393220
  29.3 5.9 %collective-permute-start.1 = (bf16[1024,512]{1,0:T(8,128)(2,1)S(1)}, bf16[1024,512]{1,0:T(8,128)(2,1)S(1)}, u32[]{:S(2)}, u32[]{:S(2)}) collective-permute-start(bf16[1024,512]{1,0:T(8,128)(2,1)S(1)} %bitcast.53), channel_id=1, source_target_pairs={{16,0},{17,1},{18,2},{19,3},{20,4},{21,5},{22,6},{23,7},{24,8},{25... | collective-permute-start | bytes 3145736 | tf_op jit(solution)/shard_map/ppermute | solution.py:92
  33.3 5.5 %collective-permute-start.2 = (bf16[64,512]{1,0:T(8,128)(2,1)S(1)}, bf16[64,512]{1,0:T(8,128)(2,1)S(1)}, u32[]{:S(2)}, u32[]{:S(2)}) collective-permute-start(bf16[64,512]{1,0:T(8,128)(2,1)S(1)} %convolution_convert_fusion), channel_id=1, source_target_pairs={{32,0},{33,1},{34,2},{35,3},{36,4},{37,5},{38,6},{39,7},{40,8},{41... | collective-permute-start | bytes 196616 | tf_op jit(solution)/shard_map/ppermute | solution.py:92
  38.8 25.1 %all-to-all-start.1 = ((bf16[16,64,640]{2,1,0:T(8,128)(2,1)}), bf16[16,64,640]{2,1,0:T(8,128)(2,1)S(1)}, u32[]{:S(2)}, u32[]{:S(2)}) async-start(bf16[16,64,640]{2,1,0:T(8,128)(2,1)} %shard_map.60), calls=%async_computation.1 | async-start | bytes 2621440 | tf_op jit(solution)/shard_map/all_to_all | solution.py:104
  42.5 22.7 %collective-permute-start.4 = (bf16[64,512]{1,0:T(8,128)(2,1)S(1)}, bf16[64,512]{1,0:T(8,128)(2,1)S(1)}, u32[]{:S(2)}, u32[]{:S(2)}) collective-permute-start(bf16[64,512]{1,0:T(8,128)(2,1)S(1)} %collective-permute-done.2), channel_id=1, source_target_pairs={{0,16},{1,17},{2,18},{3,19},{4,20},{5,21},{6,22},{7,23},{8,24},{9,... | collective-permute-start | bytes 196616 | tf_op jit(solution)/shard_map/ppermute | solution.py:92
  64.0 3.6 %collective-permute-start.5 = (bf16[1024,512]{1,0:T(8,128)(2,1)S(1)}, bf16[1024,512]{1,0:T(8,128)(2,1)S(1)}, u32[]{:S(2)}, u32[]{:S(2)}) collective-permute-start(bf16[1024,512]{1,0:T(8,128)(2,1)S(1)} %slice.71.other_ref), channel_id=1, source_target_pairs={{0,16},{1,17},{2,18},{3,19},{4,20},{5,21},{6,22},{7,23},{8,24},{9,... | collective-permute-start | bytes 3145736 | tf_op jit(solution)/shard_map/ppermute | solution.py:92
  65.3 1.0 copy-start.1
  66.3 4.2 %collective-permute-start.3 = (bf16[64,1024]{1,0:T(8,128)(2,1)S(1)}, bf16[64,1024]{1,0:T(8,128)(2,1)S(1)}, u32[]{:S(2)}, u32[]{:S(2)}) collective-permute-start(bf16[64,1024]{1,0:T(8,128)(2,1)S(1)} %fusion.27), channel_id=1, source_target_pairs={{32,0},{33,1},{34,2},{35,3},{36,4},{37,5},{38,6},{39,7},{40,8},{41... | collective-permute-start | bytes 393224 | tf_op jit(solution)/shard_map/ppermute | solution.py:92
  91.8 8.0 %collective-permute-start.7 = (bf16[1024,512]{1,0:T(8,128)(2,1)S(1)}, bf16[1024,512]{1,0:T(8,128)(2,1)S(1)}, u32[]{:S(2)}, u32[]{:S(2)}) collective-permute-start(bf16[1024,512]{1,0:T(8,128)(2,1)S(1)} %slice.73.mine_ref), channel_id=1, source_target_pairs={{16,0},{17,1},{18,2},{19,3},{20,4},{21,5},{22,6},{23,7},{24,8},{25... | collective-permute-start | bytes 3145736 | tf_op jit(solution)/shard_map/ppermute | solution.py:92
  97.7 0.7 collective-permute-start.6
  111.9 0.7 collective-permute-start.8
  124.1 0.7 collective-permute-start.9
  124.8 53.7 %slice-start = ((s8[8388608]{0:T(1024)(128)(4,1)}), s8[4194304]{0:T(1024)(128)(4,1)S(1)}, s32[]{:S(2)}) async-start(s8[8388608]{0:T(1024)(128)(4,1)} %bitcast.49), calls=%async_computation.8 | async-start | bytes 8388608
  136.6 41.9 %slice-start.1 = ((s8[8388608]{0:T(1024)(128)(4,1)}), s8[4194304]{0:T(1024)(128)(4,1)S(1)}, s32[]{:S(2)}) async-start(s8[8388608]{0:T(1024)(128)(4,1)} %bitcast.49), calls=%async_computation.9 | async-start | bytes 8388608
  136.6 29.7 %collective-permute-start.10 = (bf16[64,1024]{1,0:T(8,128)(2,1)S(1)}, bf16[64,1024]{1,0:T(8,128)(2,1)S(1)}, u32[]{:S(2)}, u32[]{:S(2)}) collective-permute-start(bf16[64,1024]{1,0:T(8,128)(2,1)S(1)} %fusion.29), channel_id=1, source_target_pairs={{32,16},{33,17},{34,18},{35,19},{36,20},{37,21},{38,22},{39,23},{4... | collective-permute-start | bytes 393224 | tf_op jit(solution)/shard_map/ppermute | solution.py:92
  180.4 14.7 %copy-start = (f32[1,4,64,1024]{3,2,1,0:T(8,128)S(1)}, f32[1,4,64,1024]{3,2,1,0:T(8,128)}, u32[]{:S(2)}) copy-start(f32[1,4,64,1024]{3,2,1,0:T(8,128)} %param.7) | copy-start | bytes 3145732

commit v4 on v3

--- a/solution.py
+++ b/solution.py
@@ -136,11 +136,11 @@
     maps = interior_map[0]
     count = maps.shape[0]
 
-    given = swap_cores(jnp.concatenate([f_rows, b_rows.astype(BF16)], 1))
-    s_rows = given[:, order:]
-    q_rows = jnp.where(first, given[:, :order], f_rows)
-    f_half = jnp.where(first, f_rows[:, :half], given[:, half:order])
+    given = swap_cores(f_rows)
+    q_rows = jnp.where(first, given, f_rows)
+    f_half = jnp.where(first, f_rows[:, :half], given[:, half:])
     odd = jnp.where(first, given[:, :half], f_rows[:, half:])
+    s_rows = from_second(b_rows.astype(BF16))
 
     def after(value, anchor):
         return lax.optimization_barrier((value, anchor))[0]
@@ -151,7 +151,6 @@
     q_half = dot(q_rows, f_mine, 1, 0).astype(BF16)
     q_half = move(q_half, lambda z, c: (z - 1, c))
     pieces = share(False, s_rows, odd, f_halves)
-    pieces, q_half = lax.optimization_barrier((pieces, q_half))
     other = swap_cores(q_half)
     pieces = exchange(pieces).reshape(order, half + 2 * chunk)
     odd = pieces[:, :half]

time: 198 us -> 194 us (0.980)
  waiting for transfers between devices: 54.8 us -> 48.7 us
  starting transfers between devices: 23.9 us -> 26.8 us
    all_to_all x1, waiting for transfers between devices: 20.9 us -> 13.6 us  [exchange(): return lax.all_to_all(pieces, 'tile', 0, 0)]
    ppermute x11 -> x12, starting transfers between devices: 20.2 us -> 22.9 us  [move(): return lax.ppermute(value, AXES, pairs)]
    ppermute x11 -> x12, waiting for transfers between devices: 33.9 us -> 35.1 us  [move(): return lax.ppermute(value, AXES, pairs)]
  transfers between devices with their start and end apart: 12 -> 13, of which waited for: 7 -> 7; matrix products, arithmetic and copies ran while one was open for 2% -> 2% of each run, Pallas kernels for 1% -> 0%
where the time goes in v4:
time: 194 us; the launch traced here: 193 us
  blocking collectives  97.7 us (50%)
  waiting for transfers between devices  48.7 us (25%)
  starting transfers between devices  26.8 us (14%)
  Pallas kernels  9.32 us (5%)
  matrix products  7.13 us (4%)
  other arithmetic  1.98 us (1%)
    all_to_all x7, blocking collectives, exchange(): return lax.all_to_all(pieces, 'tile', 0, 0)  97.7 us
    ppermute x12, waiting for transfers between devices, move(): return lax.ppermute(value, AXES, pairs)  35.1 us
    ppermute x12, starting transfers between devices, move(): return lax.ppermute(value, AXES, pairs)  22.9 us
    all_to_all x1, waiting for transfers between devices, exchange(): return lax.all_to_all(pieces, 'tile', 0, 0)  13.6 us
    dot_general x17, matrix products, dot(): lax.dot_general(left, right, (((left_dim,), (right_dim,)), ((), ())), pre...  7.13 us
  transfers between devices with their start and end apart: 13, of which 7 were waited for; matrix products, arithmetic and copies ran while one was open for 2% of the time, Pallas kernels for 0%

profile of v4, /device:TPU:1, one launch (start us, length us, event | category | flops | bytes accessed | tf_op | source)
XLA Modules:
  0.0 193.1 jit_solution(7334829714913551766)
XLA Ops:
  0.6 3.3 %collective-permute-start.1 = (bf16[64,1024]{1,0:T(8,128)(2,1)}, bf16[64,1024]{1,0:T(8,128)(2,1)S(1)}, u32[]{:S(2)}, u32[]{:S(2)}) collective-permute-start(bf16[64,1024]{1,0:T(8,128)(2,1)} %bitcast.79), channel_id=1, source_target_pairs={{0,16},{1,17},{2,18},{3,19},{4,20},{5,21},{6,22},{7,23},{8,24},{9,... | collective-permute-start | bytes 393224 | tf_op jit(solution)/shard_map/ppermute | solution.py:92
  4.0 1.2 collective-permute-done.1
  6.2 21.3 %all_to_all.40 = bf16[16,64,512]{2,1,0:T(8,128)(2,1)S(1)} all-to-all(bf16[16,64,512]{2,1,0:T(8,128)(2,1)S(1)} %shard_map.59), channel_id=1, replica_groups=mesh['tm'=16,'tile'=16] {'tile'}, dimensions={0} | all-to-all | bytes 2097152 | tf_op jit(solution)/shard_map/all_to_all | solution.py:104
  27.5 3.7 %collective-permute-start.2 = (bf16[1024,512]{1,0:T(8,128)(2,1)S(1)}, bf16[1024,512]{1,0:T(8,128)(2,1)S(1)}, u32[]{:S(2)}, u32[]{:S(2)}) collective-permute-start(bf16[1024,512]{1,0:T(8,128)(2,1)S(1)} %bitcast.53), channel_id=1, source_target_pairs={{16,0},{17,1},{18,2},{19,3},{20,4},{21,5},{22,6},{23,7},{24,8},{25... | collective-permute-start | bytes 3145736 | tf_op jit(solution)/shard_map/ppermute | solution.py:92
  31.3 1.3 collective-permute-start
  33.6 1.6 shard_map.60
  35.2 3.8 %all-to-all-start.1 = ((bf16[16,64,640]{2,1,0:T(8,128)(2,1)}), bf16[16,64,640]{2,1,0:T(8,128)(2,1)S(1)}, u32[]{:S(2)}, u32[]{:S(2)}) async-start(bf16[16,64,640]{2,1,0:T(8,128)(2,1)} %shard_map.60), calls=%async_computation.1 | async-start | bytes 2621440 | tf_op jit(solution)/shard_map/all_to_all | solution.py:104
  39.4 1.3 collective-permute-start.4
  40.7 4.2 %collective-permute-done.4 = bf16[64,512]{1,0:T(8,128)(2,1)S(1)} collective-permute-done((bf16[64,512]{1,0:T(8,128)(2,1)S(1)}, bf16[64,512]{1,0:T(8,128)(2,1)S(1)}, u32[]{:S(2)}, u32[]{:S(2)}) %collective-permute-start.4) | collective-permute-done | bytes 65568 | tf_op jit(solution)/shard_map/ppermute | solution.py:92
  44.9 1.9 %collective-permute-start.5 = (bf16[64,512]{1,0:T(8,128)(2,1)S(1)}, bf16[64,512]{1,0:T(8,128)(2,1)S(1)}, u32[]{:S(2)}, u32[]{:S(2)}) collective-permute-start(bf16[64,512]{1,0:T(8,128)(2,1)S(1)} %collective-permute-done.4), channel_id=1, source_target_pairs={{0,16},{1,17},{2,18},{3,19},{4,20},{5,21},{6,22},{7,23},{8,24},{9,... | collective-permute-start | bytes 196616 | tf_op jit(solution)/shard_map/ppermute | solution.py:92
  46.8 13.6 %all-to-all-done.1 = bf16[16,64,640]{2,1,0:T(8,128)(2,1)S(1)} async-done(((bf16[16,64,640]{2,1,0:T(8,128)(2,1)}), bf16[16,64,640]{2,1,0:T(8,128)(2,1)S(1)}, u32[]{:S(2)}, u32[]{:S(2)}) %all-to-all-start.1) | async-done | bytes 1310752 | tf_op jit(solution)/shard_map/all_to_all | solution.py:104
  60.5 1.3 collective-permute-start.6
  67.8 19.7 %all_to_all.41 = bf16[16,64,640]{2,1,0:T(8,128)(2,1)S(1)} all-to-all(bf16[16,64,640]{2,1,0:T(8,128)(2,1)S(1)} %shard_map.61), channel_id=1, replica_groups=mesh['tm'=16,'tile'=16] {'tile'}, dimensions={0} | all-to-all | bytes 2621440 | tf_op jit(solution)/shard_map/all_to_all | solution.py:104
  88.3 5.8 %collective-permute-start.8 = (bf16[1024,512]{1,0:T(8,128)(2,1)S(1)}, bf16[1024,512]{1,0:T(8,128)(2,1)S(1)}, u32[]{:S(2)}, u32[]{:S(2)}) collective-permute-start(bf16[1024,512]{1,0:T(8,128)(2,1)S(1)} %slice.63.mine_ref), channel_id=1, source_target_pairs={{16,0},{17,1},{18,2},{19,3},{20,4},{21,5},{22,6},{23,7},{24,8},{25... | collective-permute-start | bytes 3145736 | tf_op jit(solution)/shard_map/ppermute | solution.py:92
  94.9 1.5 collective-permute-done.8.other_ref
  96.9 10.7 %all_to_all.42 = bf16[16,64,128]{2,1,0:T(8,128)(2,1)S(1)} all-to-all(bf16[16,64,128]{2,1,0:T(8,128)(2,1)S(1)} %shard_map.62), channel_id=1, replica_groups=mesh['tm'=16,'tile'=16] {'tile'}, dimensions={0} | all-to-all | bytes 524288 | tf_op jit(solution)/shard_map/all_to_all | solution.py:104
  109.6 10.2 %all_to_all.43 = bf16[16,64,128]{2,1,0:T(8,128)(2,1)S(1)} all-to-all(bf16[16,64,128]{2,1,0:T(8,128)(2,1)S(1)} %shard_map.63), channel_id=1, replica_groups=mesh['tm'=16,'tile'=16] {'tile'}, dimensions={0} | all-to-all | bytes 524288 | tf_op jit(solution)/shard_map/all_to_all | solution.py:104
  121.8 10.5 %all_to_all.44 = bf16[16,64,128]{2,1,0:T(8,128)(2,1)S(1)} all-to-all(bf16[16,64,128]{2,1,0:T(8,128)(2,1)S(1)} %shard_map.64), channel_id=1, replica_groups=mesh['tm'=16,'tile'=16] {'tile'}, dimensions={0} | all-to-all | bytes 524288 | tf_op jit(solution)/shard_map/all_to_all | solution.py:104
  133.1 1.6 collective-permute-start.11
  134.6 26.5 %collective-permute-done.11.s_ref.rows_ref = bf16[64,1024]{1,0:T(8,128)(2,1)S(1)} collective-permute-done((bf16[64,1024]{1,0:T(8,128)(2,1)S(1)}, bf16[64,1024]{1,0:T(8,128)(2,1)S(1)}, u32[]{:S(2)}, u32[]{:S(2)}) %collective-permute-start.11) | collective-permute-done | bytes 131104 | tf_op jit(solution)/shard_map/ppermute | solution.py:92
  161.7 10.2 %all_to_all.45 = bf16[16,64,128]{2,1,0:T(8,128)(2,1)S(1)} all-to-all(bf16[16,64,128]{2,1,0:T(8,128)(2,1)S(1)} %shard_map.65), channel_id=1, replica_groups=mesh['tm'=16,'tile'=16] {'tile'}, dimensions={0} | all-to-all | bytes 524288 | tf_op jit(solution)/shard_map/all_to_all | solution.py:104
  173.4 1.9 %shard_map.66 = bf16[16,64,256]{2,1,0:T(8,128)(2,1)S(1)} custom-call(bf16[64,1024]{1,0:T(8,128)(2,1)S(1)} %get-tuple-element.8.sigma_ref, bf16[4,1024,1024]{2,1,0:T(8,128)(2,1)S(1)} %bitcast.51), custom_call_target="tpu_custom_call" | custom-call | flops 536870912 | bytes 8388608 | tf_op jit(solution)/shard_map/pallas_call | solution.py:202
  175.3 15.1 %all_to_all.46 = bf16[16,64,256]{2,1,0:T(8,128)(2,1)S(1)} all-to-all(bf16[16,64,256]{2,1,0:T(8,128)(2,1)S(1)} %shard_map.66), channel_id=1, replica_groups=mesh['tm'=16,'tile'=16] {'tile'}, dimensions={0} | all-to-all | bytes 1048576 | tf_op jit(solution)/shard_map/all_to_all | solution.py:104
  190.4 2.7 %shard_map.67 = f32[4,64,1024]{2,1,0:T(8,128)} custom-call(bf16[1024,256]{1,0:T(8,128)(2,1)S(1)} %bitcast.59, bf16[4,1024,1024]{2,1,0:T(8,128)(2,1)S(1)} %bitcast.52, f32[4,64,1024]{2,1,0:T(8,128)S(1)} %bitcast.60), custom_call_target="tpu_custom_call" | custom-call | flops 536870912 | bytes 8388608 | tf_op jit(solution)/shard_map/pallas_call | solution.py:212
  (62 shorter events, 17.0 us)
Async XLA Ops:
  0.6 4.5 %collective-permute-start.1 = (bf16[64,1024]{1,0:T(8,128)(2,1)}, bf16[64,1024]{1,0:T(8,128)(2,1)S(1)}, u32[]{:S(2)}, u32[]{:S(2)}) collective-permute-start(bf16[64,1024]{1,0:T(8,128)(2,1)} %bitcast.79), channel_id=1, source_target_pairs={{0,16},{1,17},{2,18},{3,19},{4,20},{5,21},{6,22},{7,23},{8,24},{9,... | collective-permute-start | bytes 393224 | tf_op jit(solution)/shard_map/ppermute | solution.py:92
  5.2 0.9 copy-start.4
  6.2 25.0 %copy-start.1 = (f32[1,64,1024]{2,1,0:T(8,128)S(1)}, f32[1,64,1024]{2,1,0:T(8,128)}, u32[]{:S(2)}) copy-start(f32[1,64,1024]{2,1,0:T(8,128)} %param.4) | copy-start | bytes 786436
  27.5 6.1 %collective-permute-start.2 = (bf16[1024,512]{1,0:T(8,128)(2,1)S(1)}, bf16[1024,512]{1,0:T(8,128)(2,1)S(1)}, u32[]{:S(2)}, u32[]{:S(2)}) collective-permute-start(bf16[1024,512]{1,0:T(8,128)(2,1)S(1)} %bitcast.53), channel_id=1, source_target_pairs={{16,0},{17,1},{18,2},{19,3},{20,4},{21,5},{22,6},{23,7},{24,8},{25... | collective-permute-start | bytes 3145736 | tf_op jit(solution)/shard_map/ppermute | solution.py:92
  31.3 2.4 %collective-permute-start = (bf16[64,1024]{1,0:T(8,128)(2,1)S(1)}, bf16[64,1024]{1,0:T(8,128)(2,1)S(1)}, u32[]{:S(2)}, u32[]{:S(2)}) collective-permute-start(bf16[64,1024]{1,0:T(8,128)(2,1)S(1)} %bitcast_convert_fusion), channel_id=1, source_target_pairs={{16,0},{17,1},{18,2},{19,3},{20,4},{21,5},{22,6},{23,7},{24,8},{25... | collective-permute-start | bytes 393224 | tf_op jit(solution)/shard_map/ppermute | solution.py:92
  35.2 3.8 %copy-start.3 = (bf16[1,64,1024]{2,1,0:T(8,128)(2,1)S(1)}, bf16[1,64,1024]{2,1,0:T(8,128)(2,1)}, u32[]{:S(2)}) copy-start(bf16[1,64,1024]{2,1,0:T(8,128)(2,1)} %param.5) | copy-start | bytes 393220
  35.2 25.2 %all-to-all-start.1 = ((bf16[16,64,640]{2,1,0:T(8,128)(2,1)}), bf16[16,64,640]{2,1,0:T(8,128)(2,1)S(1)}, u32[]{:S(2)}, u32[]{:S(2)}) async-start(bf16[16,64,640]{2,1,0:T(8,128)(2,1)} %shard_map.60), calls=%async_computation.1 | async-start | bytes 2621440 | tf_op jit(solution)/shard_map/all_to_all | solution.py:104
  39.4 5.5 %collective-permute-start.4 = (bf16[64,512]{1,0:T(8,128)(2,1)S(1)}, bf16[64,512]{1,0:T(8,128)(2,1)S(1)}, u32[]{:S(2)}, u32[]{:S(2)}) collective-permute-start(bf16[64,512]{1,0:T(8,128)(2,1)S(1)} %convolution_convert_fusion), channel_id=1, source_target_pairs={{32,0},{33,1},{34,2},{35,3},{36,4},{37,5},{38,6},{39,7},{40,8},{41... | collective-permute-start | bytes 196616 | tf_op jit(solution)/shard_map/ppermute | solution.py:92
  44.9 16.9 %collective-permute-start.5 = (bf16[64,512]{1,0:T(8,128)(2,1)S(1)}, bf16[64,512]{1,0:T(8,128)(2,1)S(1)}, u32[]{:S(2)}, u32[]{:S(2)}) collective-permute-start(bf16[64,512]{1,0:T(8,128)(2,1)S(1)} %collective-permute-done.4), channel_id=1, source_target_pairs={{0,16},{1,17},{2,18},{3,19},{4,20},{5,21},{6,22},{7,23},{8,24},{9,... | collective-permute-start | bytes 196616 | tf_op jit(solution)/shard_map/ppermute | solution.py:92
  60.5 3.6 %collective-permute-start.6 = (bf16[1024,512]{1,0:T(8,128)(2,1)S(1)}, bf16[1024,512]{1,0:T(8,128)(2,1)S(1)}, u32[]{:S(2)}, u32[]{:S(2)}) collective-permute-start(bf16[1024,512]{1,0:T(8,128)(2,1)S(1)} %slice.61.other_ref), channel_id=1, source_target_pairs={{0,16},{1,17},{2,18},{3,19},{4,20},{5,21},{6,22},{7,23},{8,24},{9,... | collective-permute-start | bytes 3145736 | tf_op jit(solution)/shard_map/ppermute | solution.py:92
  61.8 1.0 copy-start.2
  62.8 4.1 %collective-permute-start.3 = (bf16[64,1024]{1,0:T(8,128)(2,1)S(1)}, bf16[64,1024]{1,0:T(8,128)(2,1)S(1)}, u32[]{:S(2)}, u32[]{:S(2)}) collective-permute-start(bf16[64,1024]{1,0:T(8,128)(2,1)S(1)} %fusion.28), channel_id=1, source_target_pairs={{32,0},{33,1},{34,2},{35,3},{36,4},{37,5},{38,6},{39,7},{40,8},{41... | collective-permute-start | bytes 393224 | tf_op jit(solution)/shard_map/ppermute | solution.py:92
  88.3 8.0 %collective-permute-start.8 = (bf16[1024,512]{1,0:T(8,128)(2,1)S(1)}, bf16[1024,512]{1,0:T(8,128)(2,1)S(1)}, u32[]{:S(2)}, u32[]{:S(2)}) collective-permute-start(bf16[1024,512]{1,0:T(8,128)(2,1)S(1)} %slice.63.mine_ref), channel_id=1, source_target_pairs={{16,0},{17,1},{18,2},{19,3},{20,4},{21,5},{22,6},{23,7},{24,8},{25... | collective-permute-start | bytes 3145736 | tf_op jit(solution)/shard_map/ppermute | solution.py:92
  94.2 0.7 collective-permute-start.7
  108.4 0.7 collective-permute-start.9
  120.6 0.7 collective-permute-start.10
  121.3 52.1 %slice-start = ((s8[8388608]{0:T(1024)(128)(4,1)}), s8[4194304]{0:T(1024)(128)(4,1)S(1)}, s32[]{:S(2)}) async-start(s8[8388608]{0:T(1024)(128)(4,1)} %bitcast.49), calls=%async_computation.8 | async-start | bytes 8388608
  133.1 40.3 %slice-start.1 = ((s8[8388608]{0:T(1024)(128)(4,1)}), s8[4194304]{0:T(1024)(128)(4,1)S(1)}, s32[]{:S(2)}) async-start(s8[8388608]{0:T(1024)(128)(4,1)} %bitcast.49), calls=%async_computation.9 | async-start | bytes 8388608
  133.1 28.1 %collective-permute-start.11 = (bf16[64,1024]{1,0:T(8,128)(2,1)S(1)}, bf16[64,1024]{1,0:T(8,128)(2,1)S(1)}, u32[]{:S(2)}, u32[]{:S(2)}) collective-permute-start(bf16[64,1024]{1,0:T(8,128)(2,1)S(1)} %fusion.30), channel_id=1, source_target_pairs={{32,16},{33,17},{34,18},{35,19},{36,20},{37,21},{38,22},{39,23},{4... | collective-permute-start | bytes 393224 | tf_op jit(solution)/shard_map/ppermute | solution.py:92
  175.3 15.1 %copy-start = (f32[1,4,64,1024]{3,2,1,0:T(8,128)S(1)}, f32[1,4,64,1024]{3,2,1,0:T(8,128)}, u32[]{:S(2)}) copy-start(f32[1,4,64,1024]{3,2,1,0:T(8,128)} %param.7) | copy-start | bytes 3145732

commit v5 on v4

--- a/solution.py
+++ b/solution.py
@@ -18,9 +18,15 @@
     )
 
 
-def spread_rows(rows_ref, out_ref):
-    for t in range(out_ref.shape[0]):
-        out_ref[t] = rows_ref[...]
+def spread_rows(core_ref, own_ref, given_ref, out_ref):
+    half = out_ref.shape[2]
+    for core, ref in enumerate((own_ref, given_ref)):
+
+        @pl.when(core_ref[0] == core)
+        def _():
+            rows = ref[:, core * half : (core + 1) * half]
+            for t in range(out_ref.shape[0]):
+                out_ref[t] = rows
 
 
 def spread_products(with_rows, s_ref, rows_ref, mine_ref, other_ref, out_ref):
@@ -45,7 +51,7 @@
 
 
 def interior_rows(sigma_ref, maps_ref, out_ref):
-    sigma = sigma_ref[...]
+    sigma = sigma_ref[...].astype(BF16)
     count = maps_ref.shape[0]
     here, rows, width = out_ref.shape
     lane = 2 * width // count
@@ -103,9 +109,6 @@
     def exchange(pieces):
         return lax.all_to_all(pieces, "tile", 0, 0)
 
-    def gather(value):
-        return exchange(placed(spread_rows, value.shape[1])(value))
-
     def placed(kernel, width):
         return pl.pallas_call(
             kernel,
@@ -138,14 +141,20 @@
 
     given = swap_cores(f_rows)
     q_rows = jnp.where(first, given, f_rows)
-    f_half = jnp.where(first, f_rows[:, :half], given[:, half:])
     odd = jnp.where(first, given[:, :half], f_rows[:, half:])
     s_rows = from_second(b_rows.astype(BF16))
 
     def after(value, anchor):
         return lax.optimization_barrier((value, anchor))[0]
 
-    f_mine = gather(f_half).reshape(order, half)
+    whole = pl.BlockSpec(memory_space=pltpu.VMEM)
+    pieces = pl.pallas_call(
+        spread_rows,
+        in_specs=[pl.BlockSpec(memory_space=pltpu.SMEM), whole, whole],
+        out_shape=pltpu.VMEM((tiles, chunk, half), BF16),
+        compiler_params=pltpu.CompilerParams(vmem_limit_bytes=12 * 2**20),
+    )((lax.axis_index("tm") % 2).astype(jnp.int32).reshape(1), f_rows, given)
+    f_mine = exchange(pieces).reshape(order, half)
     f_halves = (f_mine, from_second(f_mine))
 
     q_half = dot(q_rows, f_mine, 1, 0).astype(BF16)
@@ -189,7 +198,6 @@
     update = fold(turn(x_rows, odd_halves), odd_halves)
     sigma = jnp.where(first, sigma, b_rows + update)
 
-    low = sigma.astype(BF16)
     params = pltpu.CompilerParams(vmem_limit_bytes=20 * 2**20)
     cost = pl.CostEstimate(
         flops=2 * count * chunk * order * order,
@@ -207,7 +215,7 @@
         out_shape=jax.ShapeDtypeStruct((tiles, chunk, count * chunk), BF16),
         compiler_params=params,
         cost_estimate=cost,
-    )(low, maps)
+    )(sigma, maps)
     v_cols = exchange(v_rows).reshape(order, count * chunk)
     interior_cov = pl.pallas_call(
         interior_sums,

time: 194 us -> 201 us (1.036)
  matrix products: 7.13 us -> 12.7 us
  starting transfers between devices: 26.8 us -> 24.4 us
  blocking collectives: 97.7 us -> 99.8 us
    dot_general x17, matrix products: 7.13 us -> 12.7 us  [dot(): lax.dot_general(left, right, (((left_dim,), (right_dim,)), ((), ())), pre...]
    ppermute x12, starting transfers between devices: 22.9 us -> 20 us  [move(): return lax.ppermute(value, AXES, pairs)]
    all_to_all x7, blocking collectives: 97.7 us -> 99.8 us  [exchange(): return lax.all_to_all(pieces, 'tile', 0, 0)]
  transfers between devices with their start and end apart: 13 -> 13, of which waited for: 7 -> 6; matrix products, arithmetic and copies ran while one was open for 2% -> 5% of each run, Pallas kernels for 0% -> 0%
where the time goes in v5:
time: 201 us; the launch traced here: 200 us
  blocking collectives  99.8 us (50%)
  waiting for transfers between devices  49.8 us (25%)
  starting transfers between devices  24.4 us (12%)
  matrix products  12.7 us (6%)
  Pallas kernels  9.3 us (5%)
  local copies, waits for them, and re-layouts  2.31 us (1%)
    all_to_all x7, blocking collectives, exchange(): return lax.all_to_all(pieces, 'tile', 0, 0)  99.8 us
    ppermute x12, waiting for transfers between devices, move(): return lax.ppermute(value, AXES, pairs)  35.3 us
    ppermute x12, starting transfers between devices, move(): return lax.ppermute(value, AXES, pairs)  20 us
    all_to_all x1, waiting for transfers between devices, exchange(): return lax.all_to_all(pieces, 'tile', 0, 0)  14.5 us
    dot_general x17, matrix products, dot(): lax.dot_general(left, right, (((left_dim,), (right_dim,)), ((), ())), pre...  12.7 us
    all_to_all x1, starting transfers between devices, exchange(): return lax.all_to_all(pieces, 'tile', 0, 0)  4.39 us
  transfers between devices with their start and end apart: 13, of which 6 were waited for; matrix products, arithmetic and copies ran while one was open for 5% of the time, Pallas kernels for 0%

profile of v5, /device:TPU:1, one launch (start us, length us, event | category | flops | bytes accessed | tf_op | source)
XLA Modules:
  0.0 199.7 jit_solution(2486301454919316535)
XLA Ops:
  0.6 3.3 %collective-permute-start.1 = (bf16[64,1024]{1,0:T(8,128)(2,1)}, bf16[64,1024]{1,0:T(8,128)(2,1)S(1)}, u32[]{:S(2)}, u32[]{:S(2)}) collective-permute-start(bf16[64,1024]{1,0:T(8,128)(2,1)} %bitcast.62), channel_id=1, source_target_pairs={{0,16},{1,17},{2,18},{3,19},{4,20},{5,21},{6,22},{7,23},{8,24},{9,... | collective-permute-start | bytes 393224 | tf_op jit(solution)/shard_map/ppermute | solution.py:98
  6.2 21.3 %all_to_all.40 = bf16[16,64,512]{2,1,0:T(8,128)(2,1)S(1)} all-to-all(bf16[16,64,512]{2,1,0:T(8,128)(2,1)S(1)} %shard_map.59), channel_id=1, replica_groups=mesh['tm'=16,'tile'=16] {'tile'}, dimensions={0} | all-to-all | bytes 2097152 | tf_op jit(solution)/shard_map/all_to_all | solution.py:110
  27.5 3.7 %collective-permute-start.2 = (bf16[1024,512]{1,0:T(8,128)(2,1)S(1)}, bf16[1024,512]{1,0:T(8,128)(2,1)S(1)}, u32[]{:S(2)}, u32[]{:S(2)}) collective-permute-start(bf16[1024,512]{1,0:T(8,128)(2,1)S(1)} %bitcast.53), channel_id=1, source_target_pairs={{16,0},{17,1},{18,2},{19,3},{20,4},{21,5},{22,6},{23,7},{24,8},{25... | collective-permute-start | bytes 3145736 | tf_op jit(solution)/shard_map/ppermute | solution.py:98
  31.2 1.3 collective-permute-start
  33.6 1.6 shard_map.60
  35.2 4.4 %all-to-all-start.1 = ((bf16[16,64,640]{2,1,0:T(8,128)(2,1)}), bf16[16,64,640]{2,1,0:T(8,128)(2,1)}, u32[]{:S(2)}, u32[]{:S(2)}) async-start(bf16[16,64,640]{2,1,0:T(8,128)(2,1)} %shard_map.60), calls=%async_computation.1 | async-start | bytes 2621440 | tf_op jit(solution)/shard_map/all_to_all | solution.py:110
  41.2 4.4 %collective-permute-done.4 = bf16[64,512]{1,0:T(8,128)(2,1)S(1)} collective-permute-done((bf16[64,512]{1,0:T(8,128)(2,1)S(1)}, bf16[64,512]{1,0:T(8,128)(2,1)S(1)}, u32[]{:S(2)}, u32[]{:S(2)}) %collective-permute-start.4) | collective-permute-done | bytes 65568 | tf_op jit(solution)/shard_map/ppermute | solution.py:98
  46.5 14.5 %all-to-all-done.1 = bf16[16,64,640]{2,1,0:T(8,128)(2,1)} async-done(((bf16[16,64,640]{2,1,0:T(8,128)(2,1)}), bf16[16,64,640]{2,1,0:T(8,128)(2,1)}, u32[]{:S(2)}, u32[]{:S(2)}) %all-to-all-start.1) | async-done | bytes 1310752 | tf_op jit(solution)/shard_map/all_to_all | solution.py:110
  62.3 1.3 collective-permute-start.6
  67.6 1.9 add_convert_fusion.other_ref
  70.3 1.9 add_convert_fusion.1.mine_ref
  73.1 21.6 %all_to_all.41 = bf16[16,64,640]{2,1,0:T(8,128)(2,1)S(1)} all-to-all(bf16[16,64,640]{2,1,0:T(8,128)(2,1)S(1)} %shard_map.61), channel_id=1, replica_groups=mesh['tm'=16,'tile'=16] {'tile'}, dimensions={0} | all-to-all | bytes 2621440 | tf_op jit(solution)/shard_map/all_to_all | solution.py:110
  95.5 4.0 %collective-permute-start.8 = (bf16[1024,512]{1,0:T(8,128)(2,1)S(1)}, bf16[1024,512]{1,0:T(8,128)(2,1)S(1)}, u32[]{:S(2)}, u32[]{:S(2)}) collective-permute-start(bf16[1024,512]{1,0:T(8,128)(2,1)S(1)} %slice.53.mine_ref), channel_id=1, source_target_pairs={{16,0},{17,1},{18,2},{19,3},{20,4},{21,5},{22,6},{23,7},{24,8},{25... | collective-permute-start | bytes 3145736 | tf_op jit(solution)/shard_map/ppermute | solution.py:98
  100.1 1.5 collective-permute-done.8.other_ref
  102.2 10.7 %all_to_all.42 = bf16[16,64,128]{2,1,0:T(8,128)(2,1)S(1)} all-to-all(bf16[16,64,128]{2,1,0:T(8,128)(2,1)S(1)} %shard_map.62), channel_id=1, replica_groups=mesh['tm'=16,'tile'=16] {'tile'}, dimensions={0} | all-to-all | bytes 524288 | tf_op jit(solution)/shard_map/all_to_all | solution.py:110
  114.9 10.4 %all_to_all.43 = bf16[16,64,128]{2,1,0:T(8,128)(2,1)S(1)} all-to-all(bf16[16,64,128]{2,1,0:T(8,128)(2,1)S(1)} %shard_map.63), channel_id=1, replica_groups=mesh['tm'=16,'tile'=16] {'tile'}, dimensions={0} | all-to-all | bytes 524288 | tf_op jit(solution)/shard_map/all_to_all | solution.py:110
  127.3 10.4 %all_to_all.44 = bf16[16,64,128]{2,1,0:T(8,128)(2,1)S(1)} all-to-all(bf16[16,64,128]{2,1,0:T(8,128)(2,1)S(1)} %shard_map.64), channel_id=1, replica_groups=mesh['tm'=16,'tile'=16] {'tile'}, dimensions={0} | all-to-all | bytes 524288 | tf_op jit(solution)/shard_map/all_to_all | solution.py:110
  138.4 1.6 collective-permute-start.11
  140.0 27.2 %collective-permute-done.11.s_ref.rows_ref = bf16[64,1024]{1,0:T(8,128)(2,1)S(1)} collective-permute-done((bf16[64,1024]{1,0:T(8,128)(2,1)S(1)}, bf16[64,1024]{1,0:T(8,128)(2,1)S(1)}, u32[]{:S(2)}, u32[]{:S(2)}) %collective-permute-start.11) | collective-permute-done | bytes 131104 | tf_op jit(solution)/shard_map/ppermute | solution.py:98
  167.7 10.2 %all_to_all.45 = bf16[16,64,128]{2,1,0:T(8,128)(2,1)S(1)} all-to-all(bf16[16,64,128]{2,1,0:T(8,128)(2,1)S(1)} %shard_map.65), channel_id=1, replica_groups=mesh['tm'=16,'tile'=16] {'tile'}, dimensions={0} | all-to-all | bytes 524288 | tf_op jit(solution)/shard_map/all_to_all | solution.py:110
  177.8 1.6 fusion.31
  179.9 2.0 shard_map.66
  181.8 15.2 %all_to_all.46 = bf16[16,64,256]{2,1,0:T(8,128)(2,1)S(1)} all-to-all(bf16[16,64,256]{2,1,0:T(8,128)(2,1)S(1)} %shard_map.66), channel_id=1, replica_groups=mesh['tm'=16,'tile'=16] {'tile'}, dimensions={0} | all-to-all | bytes 1048576 | tf_op jit(solution)/shard_map/all_to_all | solution.py:110
  197.1 2.7 %shard_map.67 = f32[4,64,1024]{2,1,0:T(8,128)} custom-call(bf16[1024,256]{1,0:T(8,128)(2,1)S(1)} %bitcast.59, bf16[4,1024,1024]{2,1,0:T(8,128)(2,1)S(1)} %bitcast.52, f32[4,64,1024]{2,1,0:T(8,128)S(1)} %bitcast.61), custom_call_target="tpu_custom_call" | custom-call | flops 536870912 | bytes 8388608 | tf_op jit(solution)/shard_map/pallas_call | solution.py:220
  (62 shorter events, 20.1 us)
Async XLA Ops:
  0.6 4.5 %collective-permute-start.1 = (bf16[64,1024]{1,0:T(8,128)(2,1)}, bf16[64,1024]{1,0:T(8,128)(2,1)S(1)}, u32[]{:S(2)}, u32[]{:S(2)}) collective-permute-start(bf16[64,1024]{1,0:T(8,128)(2,1)} %bitcast.62), channel_id=1, source_target_pairs={{0,16},{1,17},{2,18},{3,19},{4,20},{5,21},{6,22},{7,23},{8,24},{9,... | collective-permute-start | bytes 393224 | tf_op jit(solution)/shard_map/ppermute | solution.py:98
  5.2 0.9 copy-start.2
  6.2 25.1 %copy-start.4 = (f32[1,64,1024]{2,1,0:T(8,128)S(1)}, f32[1,64,1024]{2,1,0:T(8,128)}, u32[]{:S(2)}) copy-start(f32[1,64,1024]{2,1,0:T(8,128)} %param.4) | copy-start | bytes 786436
  6.2 26.4 %copy-start.3 = (bf16[1,64,1024]{2,1,0:T(8,128)(2,1)S(1)}, bf16[1,64,1024]{2,1,0:T(8,128)(2,1)}, u32[]{:S(2)}) copy-start(bf16[1,64,1024]{2,1,0:T(8,128)(2,1)} %param.5) | copy-start | bytes 393220
  27.5 6.1 %collective-permute-start.2 = (bf16[1024,512]{1,0:T(8,128)(2,1)S(1)}, bf16[1024,512]{1,0:T(8,128)(2,1)S(1)}, u32[]{:S(2)}, u32[]{:S(2)}) collective-permute-start(bf16[1024,512]{1,0:T(8,128)(2,1)S(1)} %bitcast.53), channel_id=1, source_target_pairs={{16,0},{17,1},{18,2},{19,3},{20,4},{21,5},{22,6},{23,7},{24,8},{25... | collective-permute-start | bytes 3145736 | tf_op jit(solution)/shard_map/ppermute | solution.py:98
  31.2 2.4 %collective-permute-start = (bf16[64,1024]{1,0:T(8,128)(2,1)S(1)}, bf16[64,1024]{1,0:T(8,128)(2,1)S(1)}, u32[]{:S(2)}, u32[]{:S(2)}) collective-permute-start(bf16[64,1024]{1,0:T(8,128)(2,1)S(1)} %bitcast_convert_fusion), channel_id=1, source_target_pairs={{16,0},{17,1},{18,2},{19,3},{20,4},{21,5},{22,6},{23,7},{24,8},{25... | collective-permute-start | bytes 393224 | tf_op jit(solution)/shard_map/ppermute | solution.py:98
  35.2 25.8 %all-to-all-start.1 = ((bf16[16,64,640]{2,1,0:T(8,128)(2,1)}), bf16[16,64,640]{2,1,0:T(8,128)(2,1)}, u32[]{:S(2)}, u32[]{:S(2)}) async-start(bf16[16,64,640]{2,1,0:T(8,128)(2,1)} %shard_map.60), calls=%async_computation.1 | async-start | bytes 2621440 | tf_op jit(solution)/shard_map/all_to_all | solution.py:110
  39.9 5.7 %collective-permute-start.4 = (bf16[64,512]{1,0:T(8,128)(2,1)S(1)}, bf16[64,512]{1,0:T(8,128)(2,1)S(1)}, u32[]{:S(2)}, u32[]{:S(2)}) collective-permute-start(bf16[64,512]{1,0:T(8,128)(2,1)S(1)} %convolution_convert_fusion), channel_id=1, source_target_pairs={{32,0},{33,1},{34,2},{35,3},{36,4},{37,5},{38,6},{39,7},{40,8},{41... | collective-permute-start | bytes 196616 | tf_op jit(solution)/shard_map/ppermute | solution.py:98
  45.6 18.0 %collective-permute-start.5 = (bf16[64,512]{1,0:T(8,128)(2,1)S(1)}, bf16[64,512]{1,0:T(8,128)(2,1)S(1)}, u32[]{:S(2)}, u32[]{:S(2)}) collective-permute-start(bf16[64,512]{1,0:T(8,128)(2,1)S(1)} %collective-permute-done.4), channel_id=1, source_target_pairs={{0,16},{1,17},{2,18},{3,19},{4,20},{5,21},{6,22},{7,23},{8,24},{9,... | collective-permute-start | bytes 196616 | tf_op jit(solution)/shard_map/ppermute | solution.py:98
  62.3 4.6 %collective-permute-start.6 = (bf16[1024,512]{1,0:T(8,128)(2,1)S(1)}, bf16[1024,512]{1,0:T(8,128)(2,1)S(1)}, u32[]{:S(2)}, u32[]{:S(2)}) collective-permute-start(bf16[1024,512]{1,0:T(8,128)(2,1)S(1)} %slice.51.other_ref), channel_id=1, source_target_pairs={{0,16},{1,17},{2,18},{3,19},{4,20},{5,21},{6,22},{7,23},{8,24},{9,... | collective-permute-start | bytes 3145736 | tf_op jit(solution)/shard_map/ppermute | solution.py:98
  66.2 6.0 %collective-permute-start.3 = (bf16[64,1024]{1,0:T(8,128)(2,1)S(1)}, bf16[64,1024]{1,0:T(8,128)(2,1)S(1)}, u32[]{:S(2)}, u32[]{:S(2)}) collective-permute-start(bf16[64,1024]{1,0:T(8,128)(2,1)S(1)} %fusion.28), channel_id=1, source_target_pairs={{32,0},{33,1},{34,2},{35,3},{36,4},{37,5},{38,6},{39,7},{40,8},{41... | collective-permute-start | bytes 393224 | tf_op jit(solution)/shard_map/ppermute | solution.py:98
  95.5 6.2 %collective-permute-start.8 = (bf16[1024,512]{1,0:T(8,128)(2,1)S(1)}, bf16[1024,512]{1,0:T(8,128)(2,1)S(1)}, u32[]{:S(2)}, u32[]{:S(2)}) collective-permute-start(bf16[1024,512]{1,0:T(8,128)(2,1)S(1)} %slice.53.mine_ref), channel_id=1, source_target_pairs={{16,0},{17,1},{18,2},{19,3},{20,4},{21,5},{22,6},{23,7},{24,8},{25... | collective-permute-start | bytes 3145736 | tf_op jit(solution)/shard_map/ppermute | solution.py:98
  99.5 0.7 collective-permute-start.7
  113.7 0.7 collective-permute-start.9
  126.0 0.7 collective-permute-start.10
  126.7 53.1 %slice-start = ((s8[8388608]{0:T(1024)(128)(4,1)}), s8[4194304]{0:T(1024)(128)(4,1)S(1)}, s32[]{:S(2)}) async-start(s8[8388608]{0:T(1024)(128)(4,1)} %bitcast.49), calls=%async_computation.8 | async-start | bytes 8388608
  138.4 41.4 %slice-start.1 = ((s8[8388608]{0:T(1024)(128)(4,1)}), s8[4194304]{0:T(1024)(128)(4,1)S(1)}, s32[]{:S(2)}) async-start(s8[8388608]{0:T(1024)(128)(4,1)} %bitcast.49), calls=%async_computation.9 | async-start | bytes 8388608
  138.4 28.7 %collective-permute-start.11 = (bf16[64,1024]{1,0:T(8,128)(2,1)S(1)}, bf16[64,1024]{1,0:T(8,128)(2,1)S(1)}, u32[]{:S(2)}, u32[]{:S(2)}) collective-permute-start(bf16[64,1024]{1,0:T(8,128)(2,1)S(1)} %fusion.30), channel_id=1, source_target_pairs={{32,16},{33,17},{34,18},{35,19},{36,20},{37,21},{38,22},{39,23},{4... | collective-permute-start | bytes 393224 | tf_op jit(solution)/shard_map/ppermute | solution.py:98
  179.8 2.0 %copy-start = (f32[64,1024]{1,0:T(8,128)}, f32[64,1024]{1,0:T(8,128)S(1)}, u32[]{:S(2)}) copy-start(f32[64,1024]{1,0:T(8,128)S(1)} %fusion.7.sigma_ref) | copy-start | bytes 786436
  181.8 15.2 %copy-start.1 = (f32[1,4,64,1024]{3,2,1,0:T(8,128)S(1)}, f32[1,4,64,1024]{3,2,1,0:T(8,128)}, u32[]{:S(2)}) copy-start(f32[1,4,64,1024]{3,2,1,0:T(8,128)} %param.7) | copy-start | bytes 3145732

commit v6 on v4

--- a/solution.py
+++ b/solution.py
@@ -45,7 +45,7 @@
 
 
 def interior_rows(sigma_ref, maps_ref, out_ref):
-    sigma = sigma_ref[...]
+    sigma = sigma_ref[...].astype(BF16)
     count = maps_ref.shape[0]
     here, rows, width = out_ref.shape
     lane = 2 * width // count
@@ -189,7 +189,6 @@
     update = fold(turn(x_rows, odd_halves), odd_halves)
     sigma = jnp.where(first, sigma, b_rows + update)
 
-    low = sigma.astype(BF16)
     params = pltpu.CompilerParams(vmem_limit_bytes=20 * 2**20)
     cost = pl.CostEstimate(
         flops=2 * count * chunk * order * order,
@@ -207,7 +206,7 @@
         out_shape=jax.ShapeDtypeStruct((tiles, chunk, count * chunk), BF16),
         compiler_params=params,
         cost_estimate=cost,
-    )(low, maps)
+    )(sigma, maps)
     v_cols = exchange(v_rows).reshape(order, count * chunk)
     interior_cov = pl.pallas_call(
         interior_sums,

time: 194 us -> 193 us (level)
  no operation moved by 1% of the time
where the time goes in v6:
time: 193 us; the launch traced here: 192 us
  blocking collectives  97.7 us (51%)
  waiting for transfers between devices  48.7 us (25%)
  starting transfers between devices  26.8 us (14%)
  Pallas kernels  9.34 us (5%)
  matrix products  7.13 us (4%)
    all_to_all x7, blocking collectives, exchange(): return lax.all_to_all(pieces, 'tile', 0, 0)  97.7 us
    ppermute x12, waiting for transfers between devices, move(): return lax.ppermute(value, AXES, pairs)  35.1 us
    ppermute x12, starting transfers between devices, move(): return lax.ppermute(value, AXES, pairs)  22.9 us
    all_to_all x1, waiting for transfers between devices, exchange(): return lax.all_to_all(pieces, 'tile', 0, 0)  13.6 us
    dot_general x17, matrix products, dot(): lax.dot_general(left, right, (((left_dim,), (right_dim,)), ((), ())), pre...  7.13 us
  transfers between devices with their start and end apart: 13, of which 7 were waited for; matrix products, arithmetic and copies ran while one was open for 2% of the time, Pallas kernels for 0%

profile of v6, /device:TPU:1, one launch (start us, length us, event | category | flops | bytes accessed | tf_op | source)
XLA Modules:
  0.0 192.4 jit_solution(16798692182671888794)
XLA Ops:
  0.6 3.3 %collective-permute-start.1 = (bf16[64,1024]{1,0:T(8,128)(2,1)}, bf16[64,1024]{1,0:T(8,128)(2,1)S(1)}, u32[]{:S(2)}, u32[]{:S(2)}) collective-permute-start(bf16[64,1024]{1,0:T(8,128)(2,1)} %bitcast.79), channel_id=1, source_target_pairs={{0,16},{1,17},{2,18},{3,19},{4,20},{5,21},{6,22},{7,23},{8,24},{9,... | collective-permute-start | bytes 393224 | tf_op jit(solution)/shard_map/ppermute | solution.py:92
  4.0 1.2 collective-permute-done.1
  6.2 21.3 %all_to_all.40 = bf16[16,64,512]{2,1,0:T(8,128)(2,1)S(1)} all-to-all(bf16[16,64,512]{2,1,0:T(8,128)(2,1)S(1)} %shard_map.59), channel_id=1, replica_groups=mesh['tm'=16,'tile'=16] {'tile'}, dimensions={0} | all-to-all | bytes 2097152 | tf_op jit(solution)/shard_map/all_to_all | solution.py:104
  27.5 3.7 %collective-permute-start.2 = (bf16[1024,512]{1,0:T(8,128)(2,1)S(1)}, bf16[1024,512]{1,0:T(8,128)(2,1)S(1)}, u32[]{:S(2)}, u32[]{:S(2)}) collective-permute-start(bf16[1024,512]{1,0:T(8,128)(2,1)S(1)} %bitcast.52), channel_id=1, source_target_pairs={{16,0},{17,1},{18,2},{19,3},{20,4},{21,5},{22,6},{23,7},{24,8},{25... | collective-permute-start | bytes 3145736 | tf_op jit(solution)/shard_map/ppermute | solution.py:92
  31.3 1.3 collective-permute-start
  33.6 1.6 shard_map.60
  35.2 3.8 %all-to-all-start.1 = ((bf16[16,64,640]{2,1,0:T(8,128)(2,1)}), bf16[16,64,640]{2,1,0:T(8,128)(2,1)S(1)}, u32[]{:S(2)}, u32[]{:S(2)}) async-start(bf16[16,64,640]{2,1,0:T(8,128)(2,1)} %shard_map.60), calls=%async_computation.1 | async-start | bytes 2621440 | tf_op jit(solution)/shard_map/all_to_all | solution.py:104
  39.4 1.3 collective-permute-start.4
  40.7 4.2 %collective-permute-done.4 = bf16[64,512]{1,0:T(8,128)(2,1)S(1)} collective-permute-done((bf16[64,512]{1,0:T(8,128)(2,1)S(1)}, bf16[64,512]{1,0:T(8,128)(2,1)S(1)}, u32[]{:S(2)}, u32[]{:S(2)}) %collective-permute-start.4) | collective-permute-done | bytes 65568 | tf_op jit(solution)/shard_map/ppermute | solution.py:92
  44.9 1.9 %collective-permute-start.5 = (bf16[64,512]{1,0:T(8,128)(2,1)S(1)}, bf16[64,512]{1,0:T(8,128)(2,1)S(1)}, u32[]{:S(2)}, u32[]{:S(2)}) collective-permute-start(bf16[64,512]{1,0:T(8,128)(2,1)S(1)} %collective-permute-done.4), channel_id=1, source_target_pairs={{0,16},{1,17},{2,18},{3,19},{4,20},{5,21},{6,22},{7,23},{8,24},{9,... | collective-permute-start | bytes 196616 | tf_op jit(solution)/shard_map/ppermute | solution.py:92
  46.8 13.6 %all-to-all-done.1 = bf16[16,64,640]{2,1,0:T(8,128)(2,1)S(1)} async-done(((bf16[16,64,640]{2,1,0:T(8,128)(2,1)}), bf16[16,64,640]{2,1,0:T(8,128)(2,1)S(1)}, u32[]{:S(2)}, u32[]{:S(2)}) %all-to-all-start.1) | async-done | bytes 1310752 | tf_op jit(solution)/shard_map/all_to_all | solution.py:104
  60.5 1.3 collective-permute-start.6
  67.8 19.7 %all_to_all.41 = bf16[16,64,640]{2,1,0:T(8,128)(2,1)S(1)} all-to-all(bf16[16,64,640]{2,1,0:T(8,128)(2,1)S(1)} %shard_map.61), channel_id=1, replica_groups=mesh['tm'=16,'tile'=16] {'tile'}, dimensions={0} | all-to-all | bytes 2621440 | tf_op jit(solution)/shard_map/all_to_all | solution.py:104
  88.3 5.8 %collective-permute-start.8 = (bf16[1024,512]{1,0:T(8,128)(2,1)S(1)}, bf16[1024,512]{1,0:T(8,128)(2,1)S(1)}, u32[]{:S(2)}, u32[]{:S(2)}) collective-permute-start(bf16[1024,512]{1,0:T(8,128)(2,1)S(1)} %slice.63.mine_ref), channel_id=1, source_target_pairs={{16,0},{17,1},{18,2},{19,3},{20,4},{21,5},{22,6},{23,7},{24,8},{25... | collective-permute-start | bytes 3145736 | tf_op jit(solution)/shard_map/ppermute | solution.py:92
  94.9 1.5 collective-permute-done.8.other_ref
  96.9 10.7 %all_to_all.42 = bf16[16,64,128]{2,1,0:T(8,128)(2,1)S(1)} all-to-all(bf16[16,64,128]{2,1,0:T(8,128)(2,1)S(1)} %shard_map.62), channel_id=1, replica_groups=mesh['tm'=16,'tile'=16] {'tile'}, dimensions={0} | all-to-all | bytes 524288 | tf_op jit(solution)/shard_map/all_to_all | solution.py:104
  109.6 10.2 %all_to_all.43 = bf16[16,64,128]{2,1,0:T(8,128)(2,1)S(1)} all-to-all(bf16[16,64,128]{2,1,0:T(8,128)(2,1)S(1)} %shard_map.63), channel_id=1, replica_groups=mesh['tm'=16,'tile'=16] {'tile'}, dimensions={0} | all-to-all | bytes 524288 | tf_op jit(solution)/shard_map/all_to_all | solution.py:104
  121.8 10.5 %all_to_all.44 = bf16[16,64,128]{2,1,0:T(8,128)(2,1)S(1)} all-to-all(bf16[16,64,128]{2,1,0:T(8,128)(2,1)S(1)} %shard_map.64), channel_id=1, replica_groups=mesh['tm'=16,'tile'=16] {'tile'}, dimensions={0} | all-to-all | bytes 524288 | tf_op jit(solution)/shard_map/all_to_all | solution.py:104
  133.1 1.6 collective-permute-start.11
  134.6 26.5 %collective-permute-done.11.s_ref.rows_ref = bf16[64,1024]{1,0:T(8,128)(2,1)S(1)} collective-permute-done((bf16[64,1024]{1,0:T(8,128)(2,1)S(1)}, bf16[64,1024]{1,0:T(8,128)(2,1)S(1)}, u32[]{:S(2)}, u32[]{:S(2)}) %collective-permute-start.11) | collective-permute-done | bytes 131104 | tf_op jit(solution)/shard_map/ppermute | solution.py:92
  161.7 10.2 %all_to_all.45 = bf16[16,64,128]{2,1,0:T(8,128)(2,1)S(1)} all-to-all(bf16[16,64,128]{2,1,0:T(8,128)(2,1)S(1)} %shard_map.65), channel_id=1, replica_groups=mesh['tm'=16,'tile'=16] {'tile'}, dimensions={0} | all-to-all | bytes 524288 | tf_op jit(solution)/shard_map/all_to_all | solution.py:104
  172.7 2.0 %shard_map.66 = bf16[16,64,256]{2,1,0:T(8,128)(2,1)S(1)} custom-call(f32[64,1024]{1,0:T(8,128)S(1)} %fusion.7.sigma_ref, bf16[4,1024,1024]{2,1,0:T(8,128)(2,1)S(1)} %bitcast.50), custom_call_target="tpu_custom_call" | custom-call | flops 536870912 | bytes 8388608 | tf_op jit(solution)/shard_map/pallas_call | solution.py:201
  174.7 15.1 %all_to_all.46 = bf16[16,64,256]{2,1,0:T(8,128)(2,1)S(1)} all-to-all(bf16[16,64,256]{2,1,0:T(8,128)(2,1)S(1)} %shard_map.66), channel_id=1, replica_groups=mesh['tm'=16,'tile'=16] {'tile'}, dimensions={0} | all-to-all | bytes 1048576 | tf_op jit(solution)/shard_map/all_to_all | solution.py:104
  189.7 2.7 %shard_map.67 = f32[4,64,1024]{2,1,0:T(8,128)} custom-call(bf16[1024,256]{1,0:T(8,128)(2,1)S(1)} %bitcast.58, bf16[4,1024,1024]{2,1,0:T(8,128)(2,1)S(1)} %bitcast.51, f32[4,64,1024]{2,1,0:T(8,128)S(1)} %bitcast.60), custom_call_target="tpu_custom_call" | custom-call | flops 536870912 | bytes 8388608 | tf_op jit(solution)/shard_map/pallas_call | solution.py:211
  (64 shorter events, 16.3 us)
Async XLA Ops:
  0.6 4.5 %collective-permute-start.1 = (bf16[64,1024]{1,0:T(8,128)(2,1)}, bf16[64,1024]{1,0:T(8,128)(2,1)S(1)}, u32[]{:S(2)}, u32[]{:S(2)}) collective-permute-start(bf16[64,1024]{1,0:T(8,128)(2,1)} %bitcast.79), channel_id=1, source_target_pairs={{0,16},{1,17},{2,18},{3,19},{4,20},{5,21},{6,22},{7,23},{8,24},{9,... | collective-permute-start | bytes 393224 | tf_op jit(solution)/shard_map/ppermute | solution.py:92
  5.2 0.9 copy-start.5
  6.2 25.0 %copy-start.2 = (f32[1,64,1024]{2,1,0:T(8,128)S(1)}, f32[1,64,1024]{2,1,0:T(8,128)}, u32[]{:S(2)}) copy-start(f32[1,64,1024]{2,1,0:T(8,128)} %param.4) | copy-start | bytes 786436
  27.5 6.1 %collective-permute-start.2 = (bf16[1024,512]{1,0:T(8,128)(2,1)S(1)}, bf16[1024,512]{1,0:T(8,128)(2,1)S(1)}, u32[]{:S(2)}, u32[]{:S(2)}) collective-permute-start(bf16[1024,512]{1,0:T(8,128)(2,1)S(1)} %bitcast.52), channel_id=1, source_target_pairs={{16,0},{17,1},{18,2},{19,3},{20,4},{21,5},{22,6},{23,7},{24,8},{25... | collective-permute-start | bytes 3145736 | tf_op jit(solution)/shard_map/ppermute | solution.py:92
  31.3 2.4 %collective-permute-start = (bf16[64,1024]{1,0:T(8,128)(2,1)S(1)}, bf16[64,1024]{1,0:T(8,128)(2,1)S(1)}, u32[]{:S(2)}, u32[]{:S(2)}) collective-permute-start(bf16[64,1024]{1,0:T(8,128)(2,1)S(1)} %bitcast_convert_fusion), channel_id=1, source_target_pairs={{16,0},{17,1},{18,2},{19,3},{20,4},{21,5},{22,6},{23,7},{24,8},{25... | collective-permute-start | bytes 393224 | tf_op jit(solution)/shard_map/ppermute | solution.py:92
  35.2 3.8 %copy-start.4 = (bf16[1,64,1024]{2,1,0:T(8,128)(2,1)S(1)}, bf16[1,64,1024]{2,1,0:T(8,128)(2,1)}, u32[]{:S(2)}) copy-start(bf16[1,64,1024]{2,1,0:T(8,128)(2,1)} %param.5) | copy-start | bytes 393220
  35.2 25.2 %all-to-all-start.1 = ((bf16[16,64,640]{2,1,0:T(8,128)(2,1)}), bf16[16,64,640]{2,1,0:T(8,128)(2,1)S(1)}, u32[]{:S(2)}, u32[]{:S(2)}) async-start(bf16[16,64,640]{2,1,0:T(8,128)(2,1)} %shard_map.60), calls=%async_computation.1 | async-start | bytes 2621440 | tf_op jit(solution)/shard_map/all_to_all | solution.py:104
  39.4 5.5 %collective-permute-start.4 = (bf16[64,512]{1,0:T(8,128)(2,1)S(1)}, bf16[64,512]{1,0:T(8,128)(2,1)S(1)}, u32[]{:S(2)}, u32[]{:S(2)}) collective-permute-start(bf16[64,512]{1,0:T(8,128)(2,1)S(1)} %convolution_convert_fusion), channel_id=1, source_target_pairs={{32,0},{33,1},{34,2},{35,3},{36,4},{37,5},{38,6},{39,7},{40,8},{41... | collective-permute-start | bytes 196616 | tf_op jit(solution)/shard_map/ppermute | solution.py:92
  44.9 16.9 %collective-permute-start.5 = (bf16[64,512]{1,0:T(8,128)(2,1)S(1)}, bf16[64,512]{1,0:T(8,128)(2,1)S(1)}, u32[]{:S(2)}, u32[]{:S(2)}) collective-permute-start(bf16[64,512]{1,0:T(8,128)(2,1)S(1)} %collective-permute-done.4), channel_id=1, source_target_pairs={{0,16},{1,17},{2,18},{3,19},{4,20},{5,21},{6,22},{7,23},{8,24},{9,... | collective-permute-start | bytes 196616 | tf_op jit(solution)/shard_map/ppermute | solution.py:92
  60.5 3.6 %collective-permute-start.6 = (bf16[1024,512]{1,0:T(8,128)(2,1)S(1)}, bf16[1024,512]{1,0:T(8,128)(2,1)S(1)}, u32[]{:S(2)}, u32[]{:S(2)}) collective-permute-start(bf16[1024,512]{1,0:T(8,128)(2,1)S(1)} %slice.61.other_ref), channel_id=1, source_target_pairs={{0,16},{1,17},{2,18},{3,19},{4,20},{5,21},{6,22},{7,23},{8,24},{9,... | collective-permute-start | bytes 3145736 | tf_op jit(solution)/shard_map/ppermute | solution.py:92
  61.8 1.0 copy-start.3
  62.8 4.1 %collective-permute-start.3 = (bf16[64,1024]{1,0:T(8,128)(2,1)S(1)}, bf16[64,1024]{1,0:T(8,128)(2,1)S(1)}, u32[]{:S(2)}, u32[]{:S(2)}) collective-permute-start(bf16[64,1024]{1,0:T(8,128)(2,1)S(1)} %fusion.28), channel_id=1, source_target_pairs={{32,0},{33,1},{34,2},{35,3},{36,4},{37,5},{38,6},{39,7},{40,8},{41... | collective-permute-start | bytes 393224 | tf_op jit(solution)/shard_map/ppermute | solution.py:92
  88.3 8.0 %collective-permute-start.8 = (bf16[1024,512]{1,0:T(8,128)(2,1)S(1)}, bf16[1024,512]{1,0:T(8,128)(2,1)S(1)}, u32[]{:S(2)}, u32[]{:S(2)}) collective-permute-start(bf16[1024,512]{1,0:T(8,128)(2,1)S(1)} %slice.63.mine_ref), channel_id=1, source_target_pairs={{16,0},{17,1},{18,2},{19,3},{20,4},{21,5},{22,6},{23,7},{24,8},{25... | collective-permute-start | bytes 3145736 | tf_op jit(solution)/shard_map/ppermute | solution.py:92
  94.2 0.7 collective-permute-start.7
  108.4 0.7 collective-permute-start.9
  120.6 0.7 collective-permute-start.10
  121.3 51.4 %slice-start = ((s8[8388608]{0:T(1024)(128)(4,1)}), s8[4194304]{0:T(1024)(128)(4,1)S(1)}, s32[]{:S(2)}) async-start(s8[8388608]{0:T(1024)(128)(4,1)} %bitcast.48), calls=%async_computation.8 | async-start | bytes 8388608
  133.1 39.6 %slice-start.1 = ((s8[8388608]{0:T(1024)(128)(4,1)}), s8[4194304]{0:T(1024)(128)(4,1)S(1)}, s32[]{:S(2)}) async-start(s8[8388608]{0:T(1024)(128)(4,1)} %bitcast.48), calls=%async_computation.9 | async-start | bytes 8388608
  133.1 28.1 %collective-permute-start.11 = (bf16[64,1024]{1,0:T(8,128)(2,1)S(1)}, bf16[64,1024]{1,0:T(8,128)(2,1)S(1)}, u32[]{:S(2)}, u32[]{:S(2)}) collective-permute-start(bf16[64,1024]{1,0:T(8,128)(2,1)S(1)} %fusion.30), channel_id=1, source_target_pairs={{32,16},{33,17},{34,18},{35,19},{36,20},{37,21},{38,22},{39,23},{4... | collective-permute-start | bytes 393224 | tf_op jit(solution)/shard_map/ppermute | solution.py:92
  172.7 2.0 %copy-start = (f32[64,1024]{1,0:T(8,128)}, f32[64,1024]{1,0:T(8,128)S(1)}, u32[]{:S(2)}) copy-start(f32[64,1024]{1,0:T(8,128)S(1)} %fusion.7.sigma_ref) | copy-start | bytes 786436
  174.7 15.1 %copy-start.1 = (f32[1,4,64,1024]{3,2,1,0:T(8,128)S(1)}, f32[1,4,64,1024]{3,2,1,0:T(8,128)}, u32[]{:S(2)}) copy-start(f32[1,4,64,1024]{3,2,1,0:T(8,128)} %param.7) | copy-start | bytes 3145732
